TPU v7x, 128 devices: a whole 4x4x4 slice. The times are simulated.
128 devices in a mesh: slab: 4 (over y_hi, core), col: 32 (over z, x, y_lo).
Axes of the slice: x: 4, y: 4 (y_hi: 2, y_lo: 2; y = y_hi * 2 + y_lo), z: 4, core: 2. Of those that a mesh axis runs over, the one named last changes fastest.
Arguments:
- offsets: float32 [16, 64, 3, 8192], P('slab', 'col'), may hold values from 0 to 1
- charges: float32 [16, 64, 8192], P('slab', 'col'), may hold values from -0.6 to 0.6
- check_to_equiv: float32 [98, 98], replicated, may hold values from -0.625 to 0.625
- m2m_matrix: float32 [98, 784], replicated, may hold values from -0.21875 to 0.21875
- m2l_matrix: float32 [98, 30968], replicated, may hold values from -0.046875 to 0.046875
Outputs:
- near_field: float32 [16, 64, 4, 512], P('slab', 'col')
- far_level2: float32 [98, 2048], P(None, ('slab', 'col'))
- far_level3: float32 [98, 256], P(None, ('slab', 'col'))
All inputs are finite; a program needn't handle non-finite values.
Results may differ from a plain program's by a relative error of at most 0.00014.
Values sent between devices are 32-bit elements; how exact they have to be, the bound alone decides.
A program may use at most 192 MiB of HBM per device.

v0:
```python
import jax
import jax.numpy as jnp
from jax import lax
from jax.sharding import PartitionSpec as P

Q = 64
QT = 4
P_SIZE = 5


SOFTEN = 0.0625
CHECK_SIDE = 1.45


def padded(array, sides, width):
    for axis, dim in sides:
        devices, length = (lax.axis_size(axis), array.shape[dim])
        up = [(i, (i + 1) % devices) for i in range(devices - 1)]
        down = [(j, i) for i, j in up]
        last = lax.slice_in_dim(array, length - width, length, axis=dim)
        first = lax.slice_in_dim(array, 0, width, axis=dim)
        before = lax.ppermute(last, axis, up)
        after = lax.ppermute(first, axis, down)
        array = jnp.concatenate([before, array, after], axis=dim)
    return array


def surface_table(points_side):
    picked = []
    for along_z in range(points_side):
        for along_y in range(points_side):
            for along_x in range(points_side):
                lowest = min(along_z, along_y, along_x)
                highest = max(along_z, along_y, along_x)
                if lowest == 0 or highest == points_side - 1:
                    picked.append(
                        [
                            (float(along_z) / (points_side - 1) - 0.5) * (2.0 * CHECK_SIDE) + 0.5,
                            (float(along_y) / (points_side - 1) - 0.5) * (2.0 * CHECK_SIDE) + 0.5,
                            (float(along_x) / (points_side - 1) - 0.5) * (2.0 * CHECK_SIDE) + 0.5,
                        ]
                    )
    return picked


def offset_table():
    listed = []
    for shift_z in range(-3, 4):
        for shift_y in range(-3, 4):
            for shift_x in range(-3, 4):
                if max(abs(shift_z), abs(shift_y), abs(shift_x)) >= 2:
                    listed.append([shift_z, shift_y, shift_x])
    return listed


def pair_terms(target_pos, source_pos, source_chg, shift_z, shift_y, shift_x, keep_mask):
    delta_z = target_pos[:, :, 0, :, :, None] - source_pos[:, :, 0, :, None, :] - shift_z
    delta_y = target_pos[:, :, 1, :, :, None] - source_pos[:, :, 1, :, None, :] - shift_y
    delta_x = target_pos[:, :, 2, :, :, None] - source_pos[:, :, 2, :, None, :] - shift_x
    inverse = lax.rsqrt(delta_z * delta_z + delta_y * delta_y + delta_x * delta_x + SOFTEN)
    weight = source_chg[:, :, :, None, :] * inverse * keep_mask
    cubed_term = weight * inverse * inverse
    return jnp.stack(
        [
            jnp.sum(weight, axis=-1),
            jnp.sum(cubed_term * delta_z, axis=-1),
            jnp.sum(cubed_term * delta_y, axis=-1),
            jnp.sum(cubed_term * delta_x, axis=-1),
        ],
        axis=2,
    )


def near_block(target_pos, padded_pos, padded_chg):
    z_cells = target_pos.shape[0]
    y_cells = target_pos.shape[1]
    x_cells = target_pos.shape[3]
    target_count = target_pos.shape[4]
    per_leaf = padded_pos.shape[-1]
    slot_shift = jnp.repeat(jnp.array([-1.0, 0.0, 1.0], jnp.float32), per_leaf)[None, :]
    target_slot = jnp.arange(target_count, dtype=jnp.int32)[:, None]
    source_slot = jnp.arange(3 * per_leaf, dtype=jnp.int32)[None, :] - per_leaf
    center_keep = jnp.where(target_slot == source_slot, 0.0, 1.0).astype(jnp.float32)
    ones_keep = jnp.ones_like(center_keep)
    summed = jnp.zeros((z_cells, y_cells, 4, x_cells, target_count), jnp.float32)
    for shift_z in (-1, 0, 1):
        for shift_y in (-1, 0, 1):
            window_pos = padded_pos[
                1 + shift_z : 1 + shift_z + z_cells, 1 + shift_y : 1 + shift_y + y_cells
            ]
            window_chg = padded_chg[
                1 + shift_z : 1 + shift_z + z_cells, 1 + shift_y : 1 + shift_y + y_cells
            ]
            source_pos = jnp.concatenate(
                [
                    window_pos[:, :, :, 1 + shift_x : 1 + shift_x + x_cells, :]
                    for shift_x in (-1, 0, 1)
                ],
                axis=-1,
            )
            source_chg = jnp.concatenate(
                [
                    window_chg[:, :, 1 + shift_x : 1 + shift_x + x_cells, :]
                    for shift_x in (-1, 0, 1)
                ],
                axis=-1,
            )
            keep_mask = center_keep if shift_z == 0 and shift_y == 0 else ones_keep
            summed = summed + pair_terms(
                target_pos,
                source_pos,
                source_chg,
                float(shift_z),
                float(shift_y),
                slot_shift,
                keep_mask,
            )
    return summed


def check_row(row_pos, row_chg, surface):
    delta_z = surface[:, 0, None, None] - row_pos[None, 0]
    delta_y = surface[:, 1, None, None] - row_pos[None, 1]
    delta_x = surface[:, 2, None, None] - row_pos[None, 2]
    inverse = lax.rsqrt(delta_z * delta_z + delta_y * delta_y + delta_x * delta_x)
    return jnp.sum(row_chg[None] * inverse, axis=-1)


def upward(density, m2m_matrix):
    points, z_cells, y_cells, x_cells = density.shape
    grouped = density.reshape(points, z_cells // 2, 2, y_cells // 2, 2, x_cells // 2, 2)
    grouped = jnp.transpose(grouped, (2, 4, 6, 0, 1, 3, 5)).reshape(8 * points, -1)
    parent = jnp.dot(
        m2m_matrix, grouped, precision=lax.Precision.HIGHEST, preferred_element_type=jnp.float32
    )
    return parent.reshape(points, z_cells // 2, y_cells // 2, x_cells // 2)


def interact(density_grid, owned, m2l_matrix, factor):
    points, z_cells, y_cells, x_cells = density_grid.shape
    shifts = jnp.asarray(offset_table(), jnp.int32)
    cell_z = (owned // (y_cells * x_cells))[None, :]
    cell_y = (owned // x_cells % y_cells)[None, :]
    cell_x = (owned % x_cells)[None, :]
    source_z = cell_z + shifts[:, 0:1]
    source_y = cell_y + shifts[:, 1:2]
    source_x = cell_x + shifts[:, 2:3]
    inside = (
        (source_z >= 0)
        & (source_z < z_cells)
        & (source_y >= 0)
        & (source_y < y_cells)
        & (source_x >= 0)
        & (source_x < x_cells)
    )
    parent_near = (
        (jnp.abs(jnp.floor_divide(source_z, 2) - jnp.floor_divide(cell_z, 2)) <= 1)
        & (jnp.abs(jnp.floor_divide(source_y, 2) - jnp.floor_divide(cell_y, 2)) <= 1)
        & (jnp.abs(jnp.floor_divide(source_x, 2) - jnp.floor_divide(cell_x, 2)) <= 1)
    )
    usable = (inside & parent_near).astype(jnp.float32)
    flat_index = (
        jnp.clip(source_z, 0, z_cells - 1) * (y_cells * x_cells)
        + jnp.clip(source_y, 0, y_cells - 1) * x_cells
        + jnp.clip(source_x, 0, x_cells - 1)
    )
    flat_density = density_grid.reshape(points, -1)
    picked = (
        jnp.take(flat_density, flat_index.reshape(-1), axis=1).reshape(points, shifts.shape[0], -1)
        * usable[None]
    )
    stacked = jnp.transpose(picked, (1, 0, 2)).reshape(shifts.shape[0] * points, -1)
    return factor * jnp.dot(
        m2l_matrix, stacked, precision=lax.Precision.HIGHEST, preferred_element_type=jnp.float32
    )


def body(offsets, charges, check_to_equiv, m2m_matrix, m2l_matrix):
    z_cells, y_cells, merged = charges.shape
    x_cells = merged // Q
    points = check_to_equiv.shape[0]
    positions = offsets.reshape(z_cells, y_cells, 3, x_cells, Q)
    charge_grid = charges.reshape(z_cells, y_cells, x_cells, Q)
    targets = positions[..., :QT]
    packed = jnp.concatenate([offsets, charges[:, :, None, :]], axis=2)
    bordered = padded(packed, (("slab", 0), ("col", 1)), 1)
    bordered = bordered.reshape(z_cells + 2, y_cells + 2, 4, x_cells, Q)
    bordered = jnp.pad(bordered, ((0, 0), (0, 0), (0, 0), (1, 1), (0, 0)))
    near_terms = near_block(targets, bordered[:, :, 0:3], bordered[:, :, 3])
    near_field = near_terms.reshape(z_cells, y_cells, 4, x_cells * QT)
    surface = jnp.asarray(surface_table(P_SIZE), jnp.float32)
    row_pos = positions.reshape(z_cells * y_cells, 3, x_cells, Q)
    row_chg = charge_grid.reshape(z_cells * y_cells, x_cells, Q)

    def check_bundle(bundle):
        return check_row(bundle[0], bundle[1], surface)

    checks = lax.map(check_bundle, (row_pos, row_chg))
    checks = jnp.transpose(checks, (1, 0, 2)).reshape(points, -1)
    leaf_density = jnp.dot(
        check_to_equiv, checks, precision=lax.Precision.HIGHEST, preferred_element_type=jnp.float32
    )
    leaf_density = leaf_density.reshape(points, z_cells, y_cells, x_cells)
    level_one = upward(leaf_density, m2m_matrix)
    y_parity = lax.axis_index("col") % 2
    empty_half = jnp.zeros_like(level_one)
    widened = jnp.where(
        y_parity == 0,
        jnp.concatenate([level_one, empty_half], axis=2),
        jnp.concatenate([empty_half, level_one], axis=2),
    )
    partial_sum = upward(widened, m2m_matrix)
    slab_count = lax.axis_size("slab")
    col_count = lax.axis_size("col")
    grid_z = z_cells * slab_count // 4
    grid_y = y_cells * col_count // 4
    grid_x = x_cells // 4
    own_two = grid_x // 2
    anchor = jnp.zeros((), jnp.int32)
    canvas = jnp.zeros((points, grid_z, grid_y, grid_x), jnp.float32)
    canvas = lax.dynamic_update_slice(
        canvas, partial_sum, (anchor, lax.axis_index("slab"), lax.axis_index("col") // 2, anchor)
    )
    level_two = lax.psum(canvas, ("slab", "col"))
    level_three = upward(level_two, m2m_matrix)
    device_at = lax.axis_index("slab") * col_count + lax.axis_index("col")
    owned_two = device_at * own_two + jnp.arange(own_two, dtype=jnp.int32)
    far_level2 = interact(level_two, owned_two, m2l_matrix, 1.0)
    own_three = grid_z * grid_y * grid_x // 8 // (slab_count * col_count)
    owned_three = device_at * own_three + jnp.arange(own_three, dtype=jnp.int32)
    far_level3 = interact(level_three, owned_three, m2l_matrix, 0.5)
    return (near_field, far_level2, far_level3)


def solution(mesh):
    in_specs = (P("slab", "col", None, None), P("slab", "col", None), P(), P(), P())
    out_specs = (P("slab", "col", None, None), P(None, ("slab", "col")), P(None, ("slab", "col")))
    return jax.shard_map(body, mesh=mesh, in_specs=in_specs, out_specs=out_specs, check_vma=False)
```

profile of v0, /device:TPU:1, one launch (start us, length us, event | category | flops | bytes accessed | tf_op | source)
XLA Modules:
  0.0 568.9 jit_solution(6146823032650359434)
XLA Ops:
  11.4 3.3 collective-permute-start.1
  14.8 4.8 collective-permute-start
  22.1 2.1 reshape_reshape.10
  26.1 16.8 %while.11 = (s32[]{:T(128)}, f32[8,98,128]{2,1,0:T(8,128)}, f32[8,128,64]{1,2,0:T(8,128)S(1)}, f32[8,3,128,64]{2,3,1,0:T(8,128)S(1)}, s32[]{:T(128)}, /*index=5*...) while((s32[]{:T(128)}, f32[8,98,128]{2,1,0:T(8,128)}, ...), condition=%wide.region_38.39_spmd.clone, body=%wide.region_36.38_spmd.sunk.clone.sunk | while | flops 8015620 | bytes 548153 | solution.py:198
  48.3 2.1 reshape.1158
  64.5 5.1 collective-permute-start.2
  69.6 148.1 %all-reduce.5.cloned.1.call-done = f32[98,4,16,32]{0,3,2,1:T(8,128)} async-done(((f32[98,4,16,32]{0,3,2,1:T(8,128)}), f32[98,4,16,32]{0,3,2,1:T(8,128)}) %all-reduce.5.cloned.1.call-update) | async-done | bytes 802832 | tf_op jit(solution)/shard_map/psum | solution.py:224
  219.3 2.3 reshape.1168
  221.7 2.1 convolution_bitcast_fusion.1
  226.6 17.7 %gather_fusion = f32[5056,98]{1,0:T(8,128)} fusion(f32[98,2048]{0,1:T(8,128)S(1)} %bitcast.222, s32[5120]{0:T(1024)S(1)} %copy-done.24), kind=kCustom, calls=%fused_computation | custom fusion | bytes 3984128 | tf_op jit(solution)/shard_map/jit(_take)/gather | solution.py:169
  244.2 13.8 %fusion.31 = f32[98,2]{0,1:T(2,128)} fusion(f32[30968,2]{0,1:T(2,128)S(1)} %reshape.1169, f32[98,30968]{1,0:T(8,128)} %param.15), kind=kOutput, calls=%fused_computation.152 | convolution fusion | flops 72836928 | bytes 12387984 | tf_op jit(solution)/shard_map/dot_general | solution.py:173
  258.0 3.4 fusion.28
  261.5 3.7 reshape.1166
  265.1 13.6 %convolution_bitcast_fusion.4 = f32[98,16]{0,1:T(8,128)} fusion(f32[30968,16]{0,1:T(8,128)} %reshape.1166, f32[98,30968]{1,0:T(8,128)} %param.15), kind=kOutput, calls=%fused_computation.150 | convolution fusion | flops 582693888 | bytes 14127680 | tf_op jit(solution)/shard_map/dot_general | solution.py:173
  278.7 2.6 pad_maximum_fusion
  281.3 2.0 copy.74
  283.4 4.6 reshape.1157
  288.0 20.2 %pad_slice_fusion.13 = (f32[4,2,3,128,64]{4,3,2,1,0:T(8,128)}, f32[4,2,3,128,64]{4,3,2,1,0:T(8,128)}, f32[4,2,3,128,64]{4,3,2,1,0:T(8,128)}, f32[4,2,3,128,64]{4...) fusion(f32[6,4,4,128,64]{4,3,2,1,0:T(8,128)} %reshape.1157), kind=kLoop, calls=%fused_computation.134 | loop fusion | bytes 22806528 | tf_op jit(solution)/shard_map/slice | solution.py:96
  308.2 9.8 %fusion.122 = (f32[4,2,3,128,64]{4,3,2,1,0:T(8,128)}, f32[4,2,3,128,64]{4,3,2,1,0:T(8,128)}, f32[4,2,3,128,64]{4,3,2,1,0:T(8,128)}, f32[4,2,3,128,64]{4,3,2,1,0:...) fusion(f32[6,4,4,128,64]{4,3,2,1,0:T(8,128)} %reshape.1157), kind=kLoop, calls=%fused_computation.407 | loop fusion | bytes 12582912 | tf_op jit(solution)/shard_map/slice | solution.py:96
  318.2 3.8 fusion.124
  322.1 2.2 fusion.125
  330.4 2.4 copy.129
  332.9 2.5 copy.128
  335.3 2.4 copy.127
  337.8 3.8 pad_maximum_fusion.17
  341.6 2.5 copy.126
  345.8 2.4 copy.137
  348.3 2.6 copy.136
  350.9 2.5 copy.135
  353.3 2.5 copy.134
  355.8 2.3 pad_maximum_fusion.9
  364.8 12.4 %multiply_reduce_fusion.3 = (f32[4,2,128,4]{2,3,1,0:T(4,128)S(1)}, f32[4,2,128,4]{2,3,1,0:T(4,128)S(1)}, f32[4,2,128,4]{2,3,1,0:T(4,128)S(1)}, f32[4,2,128,4]{2,...) fusion(f32[4,2,128,192]{2,3,1,0:T(8,128)S(1)} %copy-done.17, ...), kind=kLoop, calls=%fused_computation.21 | loop fusion | flops 51068928 | bytes 9683712 | tf_op jit(solution)/shard_map/reduce_sum | solution.py:65
  391.1 5.4 pad_maximum_fusion.3
  398.3 2.5 copy.105
  400.8 2.4 copy.104
  403.3 2.4 copy.103
  405.7 3.8 pad_maximum_fusion.13
  409.5 2.5 copy.102
  412.0 7.1 %pad_maximum_fusion.5 = (f32[4,2,3,128,192]{4,3,2,1,0:T(8,128)S(1)}, f32[4,2,3,128,192]{4,3,2,1,0:T(8,128)}) fusion(f32[4,2,3,128,64]{4,3,2,1,0:T(8,128)} %get-tuple-element.154, f32[4,2,3,128,64]{4,3,2,1,0:T(8,128)} %get-tuple-element.168, f32[4,2,3,128,64]{4,3,2,1,0:T(8,128)} %get-tuple-element.153, f32[4,2,3,128,64]{4,3,2,1,0:T(8,128)} %get-tuple-element.156, ...), kind=kLoop, calls=%fused_computation.68 | loop fusion | flops 2359296 | bytes 9437184 | tf_op jit(solution)/shard_map/concatenate | solution.py:94
  420.9 2.5 copy.113
  423.4 2.4 copy.112
  425.8 2.5 copy.111
  428.3 4.0 pad_maximum_fusion.15
  432.3 2.5 copy.110
  434.7 3.6 slice_bitcast_fusion.11
  438.3 2.4 copy.121
  440.8 2.4 copy.120
  443.2 2.5 copy.119
  445.7 2.5 copy.118
  448.2 12.6 %multiply_reduce_fusion.5 = (f32[4,2,128,4]{2,3,1,0:T(4,128)S(1)}, f32[4,2,128,4]{2,3,1,0:T(4,128)S(1)}, f32[4,2,128,4]{2,3,1,0:T(4,128)S(1)}, f32[4,2,128,4]{2,...) fusion(f32[4,2,128,192]{2,3,1,0:T(8,128)} %copy.105, ...), kind=kLoop, calls=%fused_computation.29 | loop fusion | flops 49496064 | bytes 9686784 | tf_op jit(solution)/shard_map/reduce_sum | solution.py:65
  496.7 7.1 %pad_maximum_fusion.1 = (f32[4,2,3,128,192]{4,3,2,1,0:T(8,128)S(1)}, f32[4,2,3,128,192]{4,3,2,1,0:T(8,128)}) fusion(f32[4,2,3,128,64]{4,3,2,1,0:T(8,128)} %get-tuple-element.147, f32[4,2,3,128,64]{4,3,2,1,0:T(8,128)} %get-tuple-element.171, f32[4,2,3,128,64]{4,3,2,1,0:T(8,128)} %get-tuple-element.146, f32[4,2,3,128,64]{4,3,2,1,0:T(8,128)} %get-tuple-element.149, ...), kind=kLoop, calls=%fused_computation.64 | loop fusion | flops 2359296 | bytes 9437184 | tf_op jit(solution)/shard_map/concatenate | solution.py:94
  505.6 2.5 copy.81
  508.0 2.4 copy.79
  510.5 2.4 copy.77
  512.9 3.8 pad_maximum_fusion.11
  516.7 2.5 copy.75
  519.2 3.6 slice_bitcast_fusion.23
  522.8 2.4 copy.89
  525.2 2.4 copy.88
  527.7 2.4 copy.87
  530.1 2.5 copy.86
  534.4 2.6 copy.97
  537.0 2.5 copy.96
  541.1 12.4 %multiply_reduce_fusion.8 = (f32[4,2,128,4]{2,3,1,0:T(4,128)S(1)}, f32[4,2,128,4]{2,3,1,0:T(4,128)S(1)}, f32[4,2,128,4]{2,3,1,0:T(4,128)S(1)}, f32[4,2,128,4]{2,...) fusion(f32[192]{0:T(256)S(1)} %sub.667, ...), kind=kLoop, calls=%fused_computation.36 | loop fusion | flops 51068928 | bytes 9683712 | tf_op jit(solution)/shard_map/reduce_sum | solution.py:65
  (309 shorter events, 129.5 us)
Async XLA Ops:
  7.2 38.5 %copy-start = (f32[98,784]{1,0:T(8,128)S(1)}, f32[98,784]{1,0:T(8,128)}, u32[]{:S(2)}) copy-start(f32[98,784]{1,0:T(8,128)} %param.14) | copy-start | bytes 921988
  7.2 12.4 %copy-start.21 = (f32[4,2,8192]{2,1,0:T(2,128)S(1)}, f32[4,2,8192]{2,1,0:T(2,128)}, u32[]{:S(2)}) copy-start(f32[4,2,8192]{2,1,0:T(2,128)} %param.12) | copy-start | bytes 786436
  7.2 13.5 %copy-start.5 = (f32[4,2,3,8192]{3,1,2,0:T(2,128)S(1)}, f32[4,2,3,8192]{3,1,2,0:T(2,128)}, u32[]{:S(2)}) copy-start(f32[4,2,3,8192]{3,1,2,0:T(2,128)} %param.11) | copy-start | bytes 2359300
  7.2 210.5 %all-reduce.5.cloned.1.call-start = ((), (), s32[]{:S(2)}) async-start(), calls=%async_computation | async-start | bytes 2097152 | tf_op jit(solution)/shard_map/psum | solution.py:224
  11.4 48.5 %collective-permute-start.1 = (f32[1,2,4,8192]{3,0,2,1:T(1,128)}, f32[1,2,4,8192]{3,0,2,1:T(1,128)}, u32[]{:S(2)}, u32[]{:S(2)}) collective-permute-start(f32[1,2,4,8192]{3,0,2,1:T(1,128)} %get-tuple-element.232), channel_id=1, source_target_pairs={{32,0},{64,32},{96,64},{33,1},{65,33},{97,65},{34,2},{66,34},{98,6... | collective-permute-start | bytes 786440 | tf_op jit(solution)/shard_map/ppermute | solution.py:23
  14.8 45.2 %collective-permute-start = (f32[1,2,4,8192]{3,0,2,1:T(1,128)}, f32[1,2,4,8192]{3,0,2,1:T(1,128)}, u32[]{:S(2)}, u32[]{:S(2)}) collective-permute-start(f32[1,2,4,8192]{3,0,2,1:T(1,128)} %get-tuple-element.231), channel_id=1, source_target_pairs={{0,32},{32,64},{64,96},{1,33},{33,65},{65,97},{2,34},{34,66},{66,9... | collective-permute-start | bytes 786440 | tf_op jit(solution)/shard_map/ppermute | solution.py:22
  20.8 5.2 copy-start.58
  20.8 5.2 copy-start.59
  20.8 5.2 copy-start.60
  26.0 18.0 %copy-start.49 = (f32[98,98]{1,0:T(8,128)S(1)}, f32[98,98]{1,0:T(8,128)}, u32[]{:S(2)}) copy-start(f32[98,98]{1,0:T(8,128)} %param.13) | copy-start | bytes 115252
  47.3 4.7 copy-start.50
  47.3 4.7 copy-start.51
  47.3 4.7 copy-start.52
  48.3 6.9 %copy-start.57 = (f32[3]{0:T(128)S(1)}, f32[3]{0:T(128)}, u32[]{:S(2)}) copy-start(f32[3]{0:T(128)} %constant.312.clone) | copy-start | bytes 40
  63.2 215.5 %collective-permute-start.3 = (f32[6,1,4,8192]{3,0,2,1:T(8,128)}, f32[6,1,4,8192]{3,0,2,1:T(8,128)}, u32[]{:S(2)}, u32[]{:S(2)}) collective-permute-start(f32[6,1,4,8192]{3,0,2,1:T(8,128)} %get-tuple-element.200), channel_id=1, source_target_pairs={{1,0},{2,1},{3,2},{4,3},{5,4},{6,5},{7,6},{8,7},{9,8},{10,9},{11,1... | collective-permute-start | bytes 2359304 | tf_op jit(solution)/shard_map/ppermute | solution.py:23
  64.5 214.2 %collective-permute-start.2 = (f32[6,1,4,8192]{3,0,2,1:T(8,128)}, f32[6,1,4,8192]{3,0,2,1:T(8,128)}, u32[]{:S(2)}, u32[]{:S(2)}) collective-permute-start(f32[6,1,4,8192]{3,0,2,1:T(8,128)} %get-tuple-element.199), channel_id=1, source_target_pairs={{0,1},{1,2},{2,3},{3,4},{4,5},{5,6},{6,7},{7,8},{8,9},{9,10},{10,1... | collective-permute-start | bytes 2359304 | tf_op jit(solution)/shard_map/ppermute | solution.py:22
  219.3 7.2 %copy-start.2 = (f32[98,4,16,32]{0,3,2,1:T(8,128)S(1)}, f32[98,4,16,32]{0,3,2,1:T(8,128)}, u32[]{:S(2)}) copy-start(f32[98,4,16,32]{0,3,2,1:T(8,128)} %all-reduce.5.cloned.1.call-done) | copy-start | bytes 2408452
  221.7 4.2 copy-start.55
  221.7 4.2 copy-start.56
  221.7 4.9 copy-start.24
  244.2 13.8 %copy-start.4 = (f32[5056,98]{1,0:T(8,128)S(1)}, f32[5056,98]{1,0:T(8,128)}, u32[]{:S(2)}) copy-start(f32[5056,98]{1,0:T(8,128)} %gather_fusion) | copy-start | bytes 5945860
  244.2 13.8 %copy-start.23 = (f32[316,16]{0,1:T(8,128)S(1)}, f32[316,16]{0,1:T(8,128)}, u32[]{:S(2)}) copy-start(f32[316,16]{0,1:T(8,128)} %copy.161) | copy-start | bytes 60676
  244.2 13.8 %copy-start.53 = (pred[316,16]{0,1:T(8,128)(4,1)S(1)}, pred[316,16]{0,1:T(8,128)(4,1)}, u32[]{:S(2)}) copy-start(pred[316,16]{0,1:T(8,128)(4,1)} %copy.150) | copy-start | bytes 15172
  308.2 9.8 %copy-start.3 = (f32[6,4,4,128,64]{4,3,2,1,0:T(8,128)S(1)}, f32[6,4,4,128,64]{4,3,2,1,0:T(8,128)}, u32[]{:S(2)}) copy-start(f32[6,4,4,128,64]{4,3,2,1,0:T(8,128)} %reshape.1157) | copy-start | bytes 9437188
  318.2 6.0 %copy-start.13 = (f32[4,2,3,128,64]{4,3,2,1,0:T(8,128)S(1)}, f32[4,2,3,128,64]{4,3,2,1,0:T(8,128)}, u32[]{:S(2)}) copy-start(f32[4,2,3,128,64]{4,3,2,1,0:T(8,128)} %get-tuple-element.166) | copy-start | bytes 2359300
  322.0 3.4 copy-start.9
  322.0 3.9 copy-start.10
  322.1 4.3 copy-start.11
  322.1 4.8 copy-start.12
  348.3 7.6 %copy-start.6 = (f32[4,2,3,128,64]{4,3,2,1,0:T(8,128)S(1)}, f32[4,2,3,128,64]{4,3,2,1,0:T(8,128)}, u32[]{:S(2)}) copy-start(f32[4,2,3,128,64]{4,3,2,1,0:T(8,128)} %get-tuple-element.161) | copy-start | bytes 2359300
  348.3 7.6 %copy-start.7 = (f32[4,2,3,128,64]{4,3,2,1,0:T(8,128)S(1)}, f32[4,2,3,128,64]{4,3,2,1,0:T(8,128)}, u32[]{:S(2)}) copy-start(f32[4,2,3,128,64]{4,3,2,1,0:T(8,128)} %get-tuple-element.162) | copy-start | bytes 2359300
  359.6 2.5 copy-start.20
  360.8 4.0 copy-start.17
  360.8 4.0 copy-start.18
  360.8 4.0 copy-start.22
  440.8 7.4 %copy-start.54 = (f32[4,192]{1,0:T(4,128)S(1)}, f32[4,192]{1,0:T(4,128)}, u32[]{:S(2)}) copy-start(f32[4,192]{1,0:T(4,128)} %fusion.114) | copy-start | bytes 9220
  534.4 5.1 copy-start.16
  534.4 6.4 %copy-start.14 = (f32[4,2,128,192]{3,2,1,0:T(8,128)S(1)}, f32[4,2,128,192]{3,2,1,0:T(8,128)}, u32[]{:S(2)}) copy-start(f32[4,2,128,192]{3,2,1,0:T(8,128)} %get-tuple-element.245) | copy-start | bytes 2359300
  537.0 4.1 copy-start.19
  556.9 3.6 copy-start.25
  556.9 3.6 copy-start.26
  556.9 3.6 copy-start.27
  556.9 3.6 copy-start.28
  556.9 3.6 copy-start.29
  556.9 3.6 copy-start.30
  556.9 3.6 copy-start.31
  556.9 3.6 copy-start.32
  557.0 3.6 copy-start.33
  557.0 3.6 copy-start.34
  557.0 3.6 copy-start.35
  557.0 3.6 copy-start.36
  557.0 3.6 copy-start.37
  557.0 3.6 copy-start.38
  557.0 3.6 copy-start.39
  557.0 3.6 copy-start.40
  557.0 3.6 copy-start.41
  557.0 3.6 copy-start.42
  557.1 3.6 copy-start.43
  557.1 3.6 copy-start.44
  557.1 3.6 copy-start.45
  557.1 3.6 copy-start.46
  557.1 3.6 copy-start.47
  557.1 3.6 copy-start.48
  557.3 4.3 copy-start.1
  (2 other events, 3.3 us)
Sparse Core Ops, SparseCore 0:
  48.4 169.2 all-reduce.4
where the time goes:
time: 579 us; the launch traced here: 569 us
  local copies, waits for them, and re-layouts  256 us (44%)
  waiting for transfers between devices  148 us (26%)
  other arithmetic  103 us (18%)
  matrix products  31.1 us (5%)
  between operations  15.8 us (3%)
  starting transfers between devices  14.6 us (3%)
    psum x1, waiting for transfers between devices, body(): level_two = lax.psum(canvas, ('slab', 'col'))  148 us
    sub x20, local copies, waits for them, and re-layouts, pair_terms(): target_pos[:, :, 0, :, :, None] - source_pos[:, :, 0, :, None, :] - shift_z  40 us
    another operation x36, local copies, waits for them, and re-layouts, pair_terms(): jnp.stack([jnp.sum(weight, axis=-1), jnp.sum(cubed_term * delta_z, axis=-...  38.7 us
    reduce_sum x3, other arithmetic, pair_terms(): jnp.sum(weight, axis=-1)  37.4 us
    slice x2, local copies, waits for them, and re-layouts, near_block(): window_pos[:, :, :, 1 + shift_x:1 + shift_x + x_cells, :]  30 us
    dot_general x2, matrix products, interact(): jnp.dot(m2l_matrix, stacked, precision=lax.Precision.HIGHEST, preferred_e...  27.4 us
    concatenate x5, other arithmetic, near_block(): jnp.concatenate([window_pos[:, :, :, 1 + shift_x:1 + shift_x + x_cells, :...  23.7 us
    sub x11, local copies, waits for them, and re-layouts, pair_terms(): target_pos[:, :, 2, :, :, None] - source_pos[:, :, 2, :, None, :] - shift_x  21.3 us
  transfers between devices with their start and end apart: 5, of which 1 were waited for; matrix products, arithmetic and copies ran while one was open for 18% of the time, Pallas kernels for 0%

commit v1 on v0

v1 whole, which is shorter than its diff:
```python
import jax
import jax.numpy as jnp
from jax import lax
from jax.experimental import pallas as pl
from jax.experimental.pallas import tpu as pltpu
from jax.sharding import PartitionSpec as P

Q = 64
QT = 4
P_SIZE = 5
NS = 98
W = 128
SOFTEN = 0.0625
CHECK_SIDE = 1.45
F32 = jnp.float32
BF16 = jnp.bfloat16

COORD = [(float(g) / (P_SIZE - 1) - 0.5) * (2.0 * CHECK_SIDE) + 0.5 for g in range(P_SIZE)]
SURFACE = [
    (a, b, c)
    for a in range(P_SIZE)
    for b in range(P_SIZE)
    for c in range(P_SIZE)
    if min(a, b, c) == 0 or max(a, b, c) == P_SIZE - 1
]
OFFSETS = [
    (z, y, x)
    for z in range(-3, 4)
    for y in range(-3, 4)
    for x in range(-3, 4)
    if max(abs(z), abs(y), abs(x)) >= 2
]
K_ALL = len(OFFSETS) * NS
CHUNK = 512
MAIN = K_ALL // CHUNK * CHUNK
REST = K_ALL - MAIN


def split(x):
    high = x.astype(BF16)
    return high, (x - high.astype(F32)).astype(BF16)


def dot(a, b):
    return jnp.dot(a, b, preferred_element_type=F32)


def dot_t(a, b):
    return lax.dot_general(a, b, (((1,), (1,)), ((), ())), preferred_element_type=F32)


def dot3(a, b, d=dot):
    ah, al = split(a)
    bh, bl = split(b)
    return d(ah, bh) + d(ah, bl) + d(al, bh)


def squares_and_checks(src_ref, check, zz, yy, xx):
    def one_row(row, carry):
        for comp, table in ((0, zz), (1, yy), (2, xx)):
            value = src_ref[row, comp]
            for g in range(P_SIZE):
                delta = COORD[g] - value
                table[g] = delta * delta
        charge = src_ref[row, 3]
        lanes = pl.ds(pl.multiple_of(row * W, W), W)
        pair = None
        for k, (a, b, c) in enumerate(SURFACE):
            if pair != (a, b):
                pair, plane = (a, b), zz[a] + yy[b]
            term = charge * lax.rsqrt(plane + xx[c])
            check[k : k + 1, lanes] = jnp.sum(term, axis=0, keepdims=True)
        return carry

    lax.fori_loop(0, 8, one_row, 0)


def pad_matrices(c2e_ref, m2m_ref, c2e, m2m):
    c2e[...] = jnp.zeros_like(c2e)
    m2m[...] = jnp.zeros_like(m2m)
    c2e[0:NS, 0:NS] = c2e_ref[...]
    for octant in range(8):
        m2m[0:NS, octant * W : octant * W + NS] = m2m_ref[:, octant * NS : (octant + 1) * NS]


def upward_two(check, c2e, m2m, grouped, parity):
    density = dot3(c2e[...], check[...])
    high, low = split(density)
    leaf = lax.broadcasted_iota(jnp.int32, (2 * W, W), 0)
    lane = lax.broadcasted_iota(jnp.int32, (2 * W, W), 1)
    cell = (lane // 64) * W + 4 * (lane % 32) + 2 * ((lane // 32) % 2)
    for bx in range(2):
        pick = jnp.where(leaf == cell + bx, 1.0, 0.0).astype(BF16)
        for bz in range(2):
            for by in range(2):
                one, two = (bz * 2 + by) * W, ((bz + 2) * 2 + by) * W
                octant = 4 * bz + 2 * by + bx
                for half, part in enumerate((high, low)):
                    both = jnp.concatenate([part[:, one : one + W], part[:, two : two + W]], axis=1)
                    grouped[half, octant * W : (octant + 1) * W, :] = dot(both, pick).astype(BF16)
    mh, ml = split(m2m[...])
    level_one = dot(mh, grouped[0]) + dot(mh, grouped[1]) + dot(ml, grouped[0])
    turned = jnp.transpose(level_one)
    total = jnp.zeros((32, W), F32)
    for bz in range(2):
        for bx in range(2):
            at = pl.multiple_of((4 * bz + 2 * parity + bx) * W, W)
            block = turned[(bz * 2 + bx) * 32 : (bz * 2 + bx + 1) * 32]
            total = total + dot3(block, m2m[:, pl.ds(at, W)], dot_t)
    return total


def shifted_sources(src_ref, moved):
    lane = lax.broadcasted_iota(jnp.int32, (Q, W), 1)

    def one(row, carry):
        for comp in range(4):
            value = src_ref[row, comp]
            left = pltpu.roll(value, 1, 1)
            right = pltpu.roll(value, W - 1, 1)
            if comp == 3:
                left = jnp.where(lane == 0, 0.0, left)
                right = jnp.where(lane == W - 1, 0.0, right)
            moved[0, row, comp] = left
            moved[1, row, comp] = value
            moved[2, row, comp] = right
        return carry

    lax.fori_loop(0, 8, one, 0)


def pair_rows(t_ref, moved, acc, zs, ys, sz, sy):
    tz, ty = zs + 1 - sz, ys + 1 - sy
    row = zs * 2 + ys
    centre = (sz == 0) & (sy == 0)
    sub = lax.broadcasted_iota(jnp.int32, (8, W), 0)
    rows = [jnp.broadcast_to(t_ref[tz, ty, k : k + 1, :], (8, W)) for k in range(12)]
    target_z = [rows[i] - sz.astype(F32) for i in range(QT)]
    target_y = [rows[QT + i] - sy.astype(F32) for i in range(QT)]
    sums = [jnp.zeros((8, W), F32) for _ in range(16)]
    for dx in range(3):
        target_x = [rows[2 * QT + i] - float(dx - 1) for i in range(QT)]
        for v in range(8):
            at = slice(8 * v, 8 * v + 8)
            z, y, x, q = [moved[dx, row, comp, at, :] for comp in range(4)]
            for i in range(QT):
                dz, dy, ddx = target_z[i] - z, target_y[i] - y, target_x[i] - x
                inverse = lax.rsqrt(dz * dz + dy * dy + (ddx * ddx + SOFTEN))
                weight = q * inverse
                if dx == 1 and v == 0:
                    weight = jnp.where((sub == i) & centre, 0.0, weight)
                cubed = weight * (inverse * inverse)
                sums[4 * i] += weight
                sums[4 * i + 1] += cubed * dz
                sums[4 * i + 2] += cubed * dy
                sums[4 * i + 3] += cubed * ddx
    for k in range(16):
        acc[tz, ty, k] += sums[k]


def pair_loop(t_ref, moved, acc, z_first, z_count, z_step, y_first, y_count, y_step):
    def one(p, carry):
        iz, iy = z_first + z_step * (p // y_count), y_first + y_step * (p % y_count)
        pair_rows(t_ref, moved, acc, iz // 3, iy // 3, 1 - iz % 3, 1 - iy % 3)
        return carry

    lax.fori_loop(0, z_count * y_count, one, 0)


def sum_rows(acc, sums, z, y):
    sums[z, y] = jnp.sum(acc[z, y], axis=1)


def densities_three(two, three, grouped, m2m):
    def gather(n, carry):
        z, y = n // 8, n % 8
        for bz in range(2):
            for by in range(2):
                for bx in range(2):
                    octant = 4 * bz + 2 * by + bx
                    grouped[pl.ds(pl.multiple_of(n * 16, 16), 16), octant * W : (octant + 1) * W] = two[
                        2 * z + bz, 2 * y + by, pl.ds(8 + bx, 16, stride=2), :
                    ]
        return carry

    lax.fori_loop(0, 16, gather, 0)
    level_three = dot3(grouped[...], m2m[...], dot_t)
    for n in range(16):
        three[n // 8, n % 8, 8:24, :] = level_three[n * 16 : (n + 1) * 16]


def stack_sources(two, three, stacked, slab, col):
    z2, y2, x2 = slab, col // 2, 16 * (col % 2)
    z3, y3, x3 = slab // 2, 4 * (slab % 2) + col // 8, 2 * (col % 8)
    sub = lax.broadcasted_iota(jnp.int32, (24, W), 0)
    lane = lax.broadcasted_iota(jnp.int32, (24, W), 1)

    def use(cell, shift, size):
        at = cell + shift
        near = jnp.abs(at // 2 - cell // 2) <= 1
        return (at >= 0) & (at < size) & near, jnp.clip(at, 0, size - 1)

    pending = None
    for o, (oz, oy, ox) in enumerate(OFFSETS):
        uz2, sz2 = use(z2, oz, 4)
        uy2, sy2 = use(y2, oy, 16)
        uz3, sz3 = use(z3, oz, 2)
        uy3, sy3 = use(y3, oy, 8)
        keep2 = jnp.where(uz2 & uy2, 1.0, 0.0).astype(F32)
        keep3 = jnp.where(uz3 & uy3, 1.0, 0.0).astype(F32)
        value = jnp.concatenate(
            [
                two[sz2, sy2, pl.ds(8 + x2 + ox, 16), :] * keep2,
                three[sz3, sy3, pl.ds(8 + x3 + ox, 8), :] * keep3,
            ],
            axis=0,
        )
        if ox == 3:
            value = jnp.where(sub % 2 == 0, value, 0.0)
        if ox == -3:
            value = jnp.where(sub % 2 == 1, value, 0.0)
        tile, start = divmod(o * NS, W)
        if start:
            value = pltpu.roll(value, start, 1)
        filled = value if pending is None else jnp.where(lane < start, pending, value)
        if start + NS >= W:
            stacked[:, tile * W : (tile + 1) * W] = filled
            pending = value if start + NS > W else None
        else:
            pending = filled
    if pending is not None:
        stacked[:, K_ALL // W * W : K_ALL // W * W + W] = jnp.where(lane < K_ALL % W, pending, 0.0)


def translate(stacked, matrix, tail):
    def one(n, total):
        at = pl.ds(pl.multiple_of(n * CHUNK, CHUNK), CHUNK)
        return total + dot3(stacked[:, at], matrix[:, at], dot_t)

    total = lax.fori_loop(0, MAIN // CHUNK, one, jnp.zeros((24, NS), F32))
    return total + dot3(stacked[:, MAIN : MAIN + REST], tail[...], dot_t)


def interleave(lines, out_ref):
    source = lax.broadcasted_iota(jnp.int32, (QT * W, QT * W), 0)
    place = lax.broadcasted_iota(jnp.int32, (QT * W, QT * W), 1)
    move = jnp.where(place == QT * (source % W) + source // W, 1.0, 0.0).astype(BF16)
    value = lines[...]
    high, low = split(value)
    lowest = (value - high.astype(F32) - low.astype(F32)).astype(BF16)
    result = dot(high, move) + dot(low, move) + dot(lowest, move)
    for row in range(8):
        out_ref[row // 2, row % 2] = result[4 * row : 4 * row + 4]


SIDES = [(s, c) for s in (-1, 0, 1) for c in (-1, 0, 1) if (s, c) != (0, 0)]


def border(step, size):
    return {-1: slice(0, 1), 0: slice(1, size + 1), 1: slice(size + 1, size + 2)}[step]


def edge(step, size):
    return {-1: slice(1, 2), 0: slice(1, size + 1), 1: slice(size, size + 1)}[step]


def whole_kernel(
    src_ref, c2e_ref, m2m_ref, m2l_ref, near_ref, far2_ref, far3_ref,
    targets, back, acc, sums, moved, lines, m2m, c2e, check, zz, yy, xx, grouped_up,
    part, arrived, two, three, grouped, stacked, matrix, tail,
    load_sem, t_send, t_recv, b_send, b_recv, p_sem, a_send, a_recv, x_send, x_recv, z_send, z_recv,
):
    slab, col = lax.axis_index("slab"), lax.axis_index("col")
    zc, xc, low_y = col // 8, (col // 2) % 4, col % 2
    place = slab * 2 + low_y

    def local_at(k):
        to = lax.rem(place + k, 8)
        return to // 2, (col // 2) * 2 + lax.rem(to, 2)

    def along_x(k):
        return slab, zc * 8 + lax.rem(xc + k, 4) * 2 + low_y

    def along_z(k):
        return slab, lax.rem(zc + k, 4) * 8 + xc * 2 + low_y

    def exists(s, c):
        return (slab + s >= 0) & (slab + s < 4) & (col + c >= 0) & (col + c < 32)

    main = pltpu.make_async_copy(m2l_ref.at[:, pl.ds(0, MAIN)], matrix, load_sem.at[0])
    rest = pltpu.make_async_copy(m2l_ref.at[:, pl.ds(MAIN, REST)], tail, load_sem.at[1])
    main.start()
    rest.start()
    targets[...] = jnp.zeros_like(targets)
    back[...] = jnp.zeros_like(back)
    two[:, :, 0:8, :] = jnp.zeros((4, 16, 8, W), F32)
    two[:, :, 40:48, :] = jnp.zeros((4, 16, 8, W), F32)

    barrier = pltpu.get_barrier_semaphore()
    others = [local_at(k) for k in range(1, 8)]
    others += [along_x(k) for k in range(1, 4)] + [along_z(k) for k in range(1, 4)]
    for other in others:
        pl.semaphore_signal(barrier, inc=1, device_id=other, device_id_type=MESH)
    outward = 2 * low_y - 1
    for s in (-1, 0, 1):
        @pl.when(exists(s, outward))
        def _(s=s):
            pl.semaphore_signal(barrier, inc=1, device_id=(slab + s, col + outward), device_id_type=MESH)

    for row in range(8):
        for comp in range(3):
            targets[row // 2 + 1, row % 2 + 1, comp * QT : (comp + 1) * QT, :] = src_ref[row, comp, 0:QT, :]
    pad_matrices(c2e_ref, m2m_ref, c2e, m2m)
    check[NS:W, :] = jnp.zeros((W - NS, 8 * W), F32)
    shifted_sources(src_ref, moved)
    acc[...] = jnp.zeros_like(acc)
    three[...] = jnp.zeros_like(three)

    more = sum(jnp.where(exists(s, outward), 1, 0) for s in (-1, 0, 1))
    pl.semaphore_wait(barrier, len(others) + more)

    def target_copy(n, s, c):
        return pltpu.make_async_remote_copy(
            src_ref=targets.at[edge(s, 4), edge(c, 2)],
            dst_ref=targets.at[border(-s, 4), border(-c, 2)],
            send_sem=t_send.at[n],
            recv_sem=t_recv.at[n],
            device_id=(slab + s, col + c),
            device_id_type=MESH,
        )

    def back_copy(n, s, c):
        return pltpu.make_async_remote_copy(
            src_ref=sums.at[border(s, 4), border(c, 2)],
            dst_ref=back.at[border(-s, 4), border(-c, 2)],
            send_sem=b_send.at[n],
            recv_sem=b_recv.at[n],
            device_id=(slab + s, col + c),
            device_id_type=MESH,
        )

    def for_sides(act):
        for n, (s, c) in enumerate(SIDES):
            @pl.when(exists(s, c))
            def _(n=n, s=s, c=c):
                act(n, s, c)

    def for_senders(act):
        for n, (s, c) in enumerate(SIDES):
            @pl.when(exists(-s, -c))
            def _(n=n, s=s, c=c):
                act(n, s, c)

    for_sides(lambda n, s, c: target_copy(n, s, c).start())

    squares_and_checks(src_ref, check, zz, yy, xx)
    part[...] = upward_two(check, c2e, m2m, grouped_up, low_y)
    theirs = pl.ds(pl.multiple_of(16 - 16 * low_y, 16), 16)
    pair_copy = pltpu.make_async_remote_copy(
        src_ref=part.at[theirs],
        dst_ref=arrived,
        send_sem=p_sem.at[0],
        recv_sem=p_sem.at[1],
        device_id=(slab, (col // 2) * 2 + 1 - low_y),
        device_id_type=MESH,
    )
    pair_copy.start()

    for_senders(lambda n, s, c: target_copy(n, s, c).wait_recv())
    pair_loop(targets, moved, acc, 0, 2, 11, 0, 6, 1)

    pair_copy.wait()
    mine = pl.ds(pl.multiple_of(16 * low_y, 16), 16)
    here = pl.ds(pl.multiple_of(8 + 16 * low_y, 8), 16)
    two[slab, col // 2, here, :] = part[mine, :] + arrived[...]

    def a_copy(k):
        block = two.at[slab, col // 2, here]
        return pltpu.make_async_remote_copy(
            src_ref=block, dst_ref=block, send_sem=a_send.at[k - 1], recv_sem=a_recv.at[k - 1],
            device_id=local_at(k), device_id_type=MESH,
        )

    def x_copy(k):
        block = two.at[:, col // 2, 8:40]
        return pltpu.make_async_remote_copy(
            src_ref=block, dst_ref=block, send_sem=x_send.at[k - 1], recv_sem=x_recv.at[k - 1],
            device_id=along_x(k), device_id_type=MESH,
        )

    def z_copy(k):
        block = two.at[:, pl.ds(zc * 4, 4), 8:40]
        return pltpu.make_async_remote_copy(
            src_ref=block, dst_ref=block, send_sem=z_send.at[k - 1], recv_sem=z_recv.at[k - 1],
            device_id=along_z(k), device_id_type=MESH,
        )

    for k in range(1, 8):
        a_copy(k).start()
    pair_loop(targets, moved, acc, 1, 10, 1, 0, 1, 5)
    for k in range(1, 8):
        a_copy(k).wait()
    for k in range(1, 4):
        x_copy(k).start()
    pair_loop(targets, moved, acc, 1, 10, 1, 5, 1, 5)

    def reduce_halo(z, y):
        sum_rows(acc, sums, z, y)

    for y in range(4):
        reduce_halo(0, y)
        reduce_halo(5, y)
    for z in range(1, 5):
        reduce_halo(z, 0)
        reduce_halo(z, 3)
    for_sides(lambda n, s, c: back_copy(n, s, c).start())
    for k in range(1, 4):
        x_copy(k).wait()
    for k in range(1, 4):
        z_copy(k).start()
    pair_loop(targets, moved, acc, 1, 10, 1, 1, 4, 1)
    for z in range(1, 5):
        for y in range(1, 3):
            sum_rows(acc, sums, z, y)
    for k in range(1, 4):
        z_copy(k).wait()

    densities_three(two, three, grouped, m2m)
    stack_sources(two, three, stacked, slab, col)
    main.wait()
    rest.wait()
    total = jnp.transpose(translate(stacked, matrix, tail))
    far2_ref[...] = total[:, 0:16]
    far3_ref[...] = 0.5 * total[:, 16:18]

    for_senders(lambda n, s, c: back_copy(n, s, c).wait_recv())
    for z in range(4):
        for y in range(2):
            value = sums[z + 1, y + 1]
            zb = {0: 0, 3: 5}.get(z)
            yb = {0: 0, 1: 3}[y]
            value = value + back[z + 1, yb]
            if zb is not None:
                value = value + back[zb, y + 1] + back[zb, yb]
            row = (z * 2 + y) * 4
            for i in range(QT):
                lines[row : row + 4, i * W : (i + 1) * W] = value[4 * i : 4 * i + 4]
    interleave(lines, near_ref)
    for_sides(lambda n, s, c: target_copy(n, s, c).wait_send())
    for_sides(lambda n, s, c: back_copy(n, s, c).wait_send())


MESH = pl.DeviceIdType.MESH
VMEM = pl.BlockSpec(memory_space=pltpu.VMEM)


def scratch(*shape, dtype=F32):
    return pltpu.VMEM(shape, dtype)


def body(offsets, charges, check_to_equiv, m2m_matrix, m2l_matrix):
    packed = jnp.concatenate([offsets, charges[:, :, None, :]], axis=2)
    sources = jnp.swapaxes(packed.reshape(8, 4, W, Q), 2, 3)
    dma = pltpu.SemaphoreType.DMA
    return pl.pallas_call(
        whole_kernel,
        name="whole",
        out_shape=(
            jax.ShapeDtypeStruct((4, 2, 4, W * QT), F32),
            jax.ShapeDtypeStruct((NS, 16), F32),
            jax.ShapeDtypeStruct((NS, 2), F32),
        ),
        in_specs=[VMEM] * 3 + [pl.BlockSpec(memory_space=pl.ANY)],
        out_specs=(VMEM, VMEM, VMEM),
        scratch_shapes=[
            scratch(6, 4, 16, W),
            scratch(6, 4, 16, W),
            scratch(6, 4, 16, 8, W),
            scratch(6, 4, 16, W),
            scratch(3, 8, 4, Q, W),
            scratch(32, QT * W),
            scratch(W, 8 * W),
            scratch(W, W),
            scratch(W, 8 * W),
            scratch(P_SIZE, Q, W),
            scratch(P_SIZE, Q, W),
            scratch(P_SIZE, Q, W),
            scratch(2, 8 * W, W, dtype=BF16),
            scratch(32, W),
            scratch(16, W),
            scratch(4, 16, 48, W),
            scratch(2, 8, 40, W),
            scratch(256, 8 * W),
            scratch(24, (K_ALL + W - 1) // W * W),
            scratch(NS, MAIN),
            scratch(NS, REST),
            dma((2,)),
            dma((8,)),
            dma((8,)),
            dma((8,)),
            dma((8,)),
            dma((2,)),
            dma((7,)),
            dma((7,)),
            dma((3,)),
            dma((3,)),
            dma((3,)),
            dma((3,)),
        ],
        compiler_params=pltpu.CompilerParams(
            vmem_limit_bytes=58 * 1024 * 1024, collective_id=0, has_side_effects=True
        ),
        cost_estimate=pl.CostEstimate(flops=400000000, bytes_accessed=16000000, transcendentals=0),
    )(sources, check_to_equiv, m2m_matrix, m2l_matrix)


def solution(mesh):
    in_specs = (P("slab", "col", None, None), P("slab", "col", None), P(), P(), P())
    out_specs = (P("slab", "col", None, None), P(None, ("slab", "col")), P(None, ("slab", "col")))
    return jax.shard_map(body, mesh=mesh, in_specs=in_specs, out_specs=out_specs, check_vma=False)
```

time: 579 us -> 69.2 us (0.12); the launches traced: 569 us -> 68.9 us
  local copies, waits for them, and re-layouts: 256 us -> 8.41 us
  waiting for transfers between devices: 148 us -> 0 us
  other arithmetic: 103 us -> 1.06 us
  Pallas kernels: 0 us -> 58.8 us
  matrix products: 31.1 us -> 0 us
  between operations: 15.8 us -> 0.66 us
  starting transfers between devices: 14.6 us -> 0 us
    psum x1 -> x0, waiting for transfers between devices: 148 us -> none  [body(): level_two = lax.psum(canvas, ('slab', 'col'))]
    sub x49 -> x0, local copies, waits for them, and re-layouts: 82.7 us -> none  [the longest x20 40 us: pair_terms(): target_pos[:, :, 0, :, :, None] - source_pos[:, :, 0, :, None, :] - shift_z]
    pallas_call x0 -> x1, Pallas kernels: none -> 58.8 us  [body(): pl.pallas_call(whole_kernel, name='whole', out_shape=(jax.ShapeDtypeStruc...]
    reduce_sum x11 -> x0, other arithmetic: 48.9 us -> none  [the longest x3 37.4 us: pair_terms(): jnp.sum(weight, axis=-1)]
    concatenate x12 -> x0, other arithmetic: 45 us -> none  [the longest x5 23.7 us: near_block(): jnp.concatenate([window_pos[:, :, :, 1 + shift_x:1 + shift_x + x_cells, :...]
    another operation x38 -> x0, local copies, waits for them, and re-layouts: 41.9 us -> none  [the longest x36 38.7 us: pair_terms(): jnp.stack([jnp.sum(weight, axis=-1), jnp.sum(cubed_term * delta_z, axis=-...]
    slice x5 -> x0, local copies, waits for them, and re-layouts: 37.5 us -> none  [the longest x2 30 us: near_block(): window_pos[:, :, :, 1 + shift_x:1 + shift_x + x_cells, :]]
    dot_general x6 -> x0, matrix products: 31.1 us -> none  [the longest x2 27.4 us: interact(): jnp.dot(m2l_matrix, stacked, precision=lax.Precision.HIGHEST, preferred_e...]
  transfers between devices with their start and end apart: 5 -> 0, of which waited for: 1 -> 0; matrix products, arithmetic and copies ran while one was open for 18% -> 0% of each run, Pallas kernels for 0% -> 0%
where the time goes in v1:
time: 69.2 us; the launch traced here: 68.9 us
  Pallas kernels  58.8 us (85%)
  local copies, waits for them, and re-layouts  8.41 us (12%)
  other arithmetic  1.06 us (2%)
    pallas_call x1, Pallas kernels, body(): pl.pallas_call(whole_kernel, name='whole', out_shape=(jax.ShapeDtypeStruc...  58.8 us
    pallas_call x2, local copies, waits for them, and re-layouts, body(): pl.pallas_call(whole_kernel, name='whole', out_shape=(jax.ShapeDtypeStruc...  2.92 us
    concatenate x4, local copies, waits for them, and re-layouts, body(): packed = jnp.concatenate([offsets, charges[:, :, None, :]], axis=2)  2.83 us
    unnamed x2, local copies, waits for them, and re-layouts  2.66 us

profile of v1, /device:TPU:1, one launch (start us, length us, event | category | flops | bytes accessed | tf_op | source)
XLA Modules:
  0.0 68.9 jit_solution(17322097424296980113)
XLA Ops:
  0.6 1.2 %copy.10 = f32[4,2,3,8192]{3,1,0,2:T(2,128)S(1)} copy(f32[4,2,3,8192]{3,1,2,0:T(2,128)} %param.5) | data formatting | bytes 1572864 | tf_op args[0]
  1.8 0.9 %concatenate.8 = f32[8,3,128,64]{3,2,0,1:T(8,128)S(1)} reshape(f32[4,2,3,8192]{3,1,0,2:T(2,128)S(1)} %copy.10) | data formatting | bytes 1572864 | tf_op jit(solution)/shard_map/concatenate | solution.py:462
  2.7 0.5 copy.11
  3.2 1.3 %concatenate.9 = f32[8,1,128,64]{3,2,0,1:T(8,128)S(1)} reshape(f32[4,2,8192]{2,1,0:T(2,128)} %param.6) | data formatting | bytes 524288 | tf_op jit(solution)/shard_map/concatenate | solution.py:462
  4.5 0.2 copy.12
  4.7 1.1 %maximum_bitcast_fusion.src_ref = f32[8,4,64,128]{3,2,1,0:T(8,128)} fusion(f32[8,1,128,64]{2,3,1,0:T(8,128)S(1)} %copy.12, f32[8,3,128,64]{2,3,1,0:T(8,128)S(1)} %copy.11), kind=kLoop, calls=%fused_computation | loop fusion | flops 262144 | bytes 2097152 | tf_op jit(solution)/shard_map/transpose | solution.py:463
  5.7 58.8 %whole.1 = (f32[4,2,4,512]{3,2,1,0:T(4,128)}, f32[98,16]{1,0:T(8,128)}, f32[98,2]{1,0:T(8,128)}) custom-call(f32[8,4,64,128]{3,2,1,0:T(8,128)} %maximum_bitcast_fusion.src_ref, f32[98,98]{1,0:T(8,128)} %c2e_ref.1, f32[98,784]{1,0:T(8,128)} %m2m_ref.1, f32[98,30968]{1,0:T(8,128)} %m2l_ref.1), custom_call_target="tpu_custom_call" | custom-call | flops 400000000 | bytes 16000000 | tf_op jit(solution)/shard_map/whole/pallas_call | solution.py:465
  64.5 1.5 %copy.13 = f32[98,16]{0,1:T(8,128)} copy(f32[98,16]{1,0:T(8,128)} %get-tuple-element.7) | data formatting | bytes 12544 | tf_op jit(solution)/shard_map/whole/pallas_call | solution.py:465
  66.0 1.4 %copy.14 = f32[98,2]{0,1:T(2,128)} copy(f32[98,2]{1,0:T(8,128)} %get-tuple-element.8) | data formatting | bytes 1568 | tf_op jit(solution)/shard_map/whole/pallas_call | solution.py:465
  67.4 1.5 %copy.16 = f32[4,2,4,512]{3,2,1,0:T(4,128)} copy(f32[4,2,4,512]{3,2,1,0:T(4,128)} %get-tuple-element.12) | data formatting | bytes 131072

commit v2 on v1

--- a/solution.py
+++ b/solution.py
@@ -31,9 +31,10 @@
     if max(abs(z), abs(y), abs(x)) >= 2
 ]
 K_ALL = len(OFFSETS) * NS
-CHUNK = 512
-MAIN = K_ALL // CHUNK * CHUNK
-REST = K_ALL - MAIN
+TILES = 140
+CHUNK = 28 * W
+LAST = K_ALL // W * W
+REST = K_ALL - LAST
 
 
 def split(x):
@@ -88,9 +89,9 @@
     high, low = split(density)
     leaf = lax.broadcasted_iota(jnp.int32, (2 * W, W), 0)
     lane = lax.broadcasted_iota(jnp.int32, (2 * W, W), 1)
-    cell = (lane // 64) * W + 4 * (lane % 32) + 2 * ((lane // 32) % 2)
+    cell = (lane // 64) * W + 2 * (lane % 32) + (lane // 32) % 2
     for bx in range(2):
-        pick = jnp.where(leaf == cell + bx, 1.0, 0.0).astype(BF16)
+        pick = jnp.where(leaf == cell + 64 * bx, 1.0, 0.0).astype(BF16)
         for bz in range(2):
             for by in range(2):
                 one, two = (bz * 2 + by) * W, ((bz + 2) * 2 + by) * W
@@ -110,14 +111,18 @@
     return total
 
 
-def shifted_sources(src_ref, moved):
+def arrange_sources(positions, charge, moved):
     lane = lax.broadcasted_iota(jnp.int32, (Q, W), 1)
 
     def one(row, carry):
+        z, y = row // 2, row % 2
         for comp in range(4):
-            value = src_ref[row, comp]
-            left = pltpu.roll(value, 1, 1)
-            right = pltpu.roll(value, W - 1, 1)
+            line = positions[z, comp, pl.ds(y, 1), :] if comp < 3 else charge[z, pl.ds(y, 1), :]
+            turned = jnp.transpose(line.reshape(Q, W))
+            value = jnp.concatenate([turned[0:Q], turned[Q : 2 * Q]], axis=1)
+            half = pltpu.roll(value, 64, 1)
+            left = jnp.where(lane < 64, pltpu.roll(value, 65, 1), half)
+            right = jnp.where(lane < 64, half, pltpu.roll(value, 63, 1))
             if comp == 3:
                 left = jnp.where(lane == 0, 0.0, left)
                 right = jnp.where(lane == W - 1, 0.0, right)
@@ -158,13 +163,13 @@
         acc[tz, ty, k] += sums[k]
 
 
-def pair_loop(t_ref, moved, acc, z_first, z_count, z_step, y_first, y_count, y_step):
+def pair_loop(t_ref, moved, acc, z_first, z_count, z_step, y_first, y_count, y_step=1):
     def one(p, carry):
         iz, iy = z_first + z_step * (p // y_count), y_first + y_step * (p % y_count)
         pair_rows(t_ref, moved, acc, iz // 3, iy // 3, 1 - iz % 3, 1 - iy % 3)
         return carry
 
-    lax.fori_loop(0, z_count * y_count, one, 0)
+    lax.fori_loop(0, z_count * y_count, one, 0, unroll=2)
 
 
 def sum_rows(acc, sums, z, y):
@@ -200,51 +205,74 @@
         near = jnp.abs(at // 2 - cell // 2) <= 1
         return (at >= 0) & (at < size) & near, jnp.clip(at, 0, size - 1)
 
-    pending = None
-    for o, (oz, oy, ox) in enumerate(OFFSETS):
-        uz2, sz2 = use(z2, oz, 4)
-        uy2, sy2 = use(y2, oy, 16)
-        uz3, sz3 = use(z3, oz, 2)
-        uy3, sy3 = use(y3, oy, 8)
-        keep2 = jnp.where(uz2 & uy2, 1.0, 0.0).astype(F32)
-        keep3 = jnp.where(uz3 & uy3, 1.0, 0.0).astype(F32)
-        value = jnp.concatenate(
-            [
-                two[sz2, sy2, pl.ds(8 + x2 + ox, 16), :] * keep2,
-                three[sz3, sy3, pl.ds(8 + x3 + ox, 8), :] * keep3,
-            ],
-            axis=0,
-        )
-        if ox == 3:
-            value = jnp.where(sub % 2 == 0, value, 0.0)
-        if ox == -3:
-            value = jnp.where(sub % 2 == 1, value, 0.0)
-        tile, start = divmod(o * NS, W)
-        if start:
-            value = pltpu.roll(value, start, 1)
-        filled = value if pending is None else jnp.where(lane < start, pending, value)
-        if start + NS >= W:
-            stacked[:, tile * W : (tile + 1) * W] = filled
-            pending = value if start + NS > W else None
-        else:
-            pending = filled
-    if pending is not None:
-        stacked[:, K_ALL // W * W : K_ALL // W * W + W] = jnp.where(lane < K_ALL % W, pending, 0.0)
-
-
-def translate(stacked, matrix, tail):
+    for gz in range(-3, 4):
+        chosen = [o for o, shift in enumerate(OFFSETS) if shift[0] == gz]
+
+        @pl.when((slab + gz >= 0) & (slab + gz < 4))
+        def _(chosen=chosen):
+            pending = None
+            for o in chosen:
+                _, oy, ox = OFFSETS[o]
+                oz = OFFSETS[o][0]
+                uz2, sz2 = use(z2, oz, 4)
+                uy2, sy2 = use(y2, oy, 16)
+                uz3, sz3 = use(z3, oz, 2)
+                uy3, sy3 = use(y3, oy, 8)
+                keep2 = jnp.where(uz2 & uy2, 1.0, 0.0).astype(F32)
+                keep3 = jnp.where(uz3 & uy3, 1.0, 0.0).astype(F32)
+                value = jnp.concatenate(
+                    [
+                        two[sz2, sy2, pl.ds(8 + x2 + ox, 16), :] * keep2,
+                        three[sz3, sy3, pl.ds(8 + x3 + ox, 8), :] * keep3,
+                    ],
+                    axis=0,
+                )
+                if ox == 3:
+                    value = jnp.where(sub % 2 == 0, value, 0.0)
+                if ox == -3:
+                    value = jnp.where(sub % 2 == 1, value, 0.0)
+                tile, start = divmod(o * NS, W)
+                at = slice(tile * W, (tile + 1) * W)
+                if start:
+                    value = pltpu.roll(value, start, 1)
+                    if pending is None:
+                        pending = stacked[:, at]
+                    filled = jnp.where(lane < start, pending, value)
+                else:
+                    filled = value
+                if start + NS >= W:
+                    stacked[:, at] = filled
+                    pending = value if start + NS > W else None
+                else:
+                    pending = filled
+            if pending is not None:
+                tile, end = divmod((chosen[-1] + 1) * NS, W)
+                stacked[:, tile * W : (tile + 1) * W] = jnp.where(lane < end, pending, 0.0)
+
+
+def far_terms(matrix, sources):
+    mh, ml = split(matrix)
+    sh, sl = split(sources)
+    return dot_t(mh, jnp.concatenate([sh, sl], axis=0)) + dot_t(ml, jnp.concatenate([sh, jnp.zeros_like(sl)], axis=0))
+
+
+def translate(stacked, matrix, tail, first):
     def one(n, total):
-        at = pl.ds(pl.multiple_of(n * CHUNK, CHUNK), CHUNK)
-        return total + dot3(stacked[:, at], matrix[:, at], dot_t)
-
-    total = lax.fori_loop(0, MAIN // CHUNK, one, jnp.zeros((24, NS), F32))
-    return total + dot3(stacked[:, MAIN : MAIN + REST], tail[...], dot_t)
-
-
-def interleave(lines, out_ref):
+        here = pl.ds(pl.multiple_of(n * CHUNK, W), CHUNK)
+        there = pl.ds(pl.multiple_of(first + n * CHUNK, W), CHUNK)
+        return total + far_terms(matrix[:, here], stacked[:, there])
+
+    total = far_terms(tail[...], stacked[:, LAST:K_ALL])
+    total = lax.fori_loop(0, TILES * W // CHUNK, one, total)
+    return total[:, 0:24] + total[:, 24:48]
+
+
+def finish_kernel(lines, far, out_ref, far2_ref, far3_ref):
+    far2_ref[...] = far[0:16]
+    far3_ref[...] = 0.5 * far[16:18]
     source = lax.broadcasted_iota(jnp.int32, (QT * W, QT * W), 0)
     place = lax.broadcasted_iota(jnp.int32, (QT * W, QT * W), 1)
-    move = jnp.where(place == QT * (source % W) + source // W, 1.0, 0.0).astype(BF16)
+    move = jnp.where(place == QT * (2 * (source % 64) + source // 64 % 2) + source // W, 1.0, 0.0).astype(BF16)
     value = lines[...]
     high, low = split(value)
     lowest = (value - high.astype(F32) - low.astype(F32)).astype(BF16)
@@ -265,8 +293,8 @@
 
 
 def whole_kernel(
-    src_ref, c2e_ref, m2m_ref, m2l_ref, near_ref, far2_ref, far3_ref,
-    targets, back, acc, sums, moved, lines, m2m, c2e, check, zz, yy, xx, grouped_up,
+    positions_ref, charges_ref, c2e_ref, m2m_ref, m2l_ref, lines, far,
+    positions, charge, c2e_in, m2m_in, targets, back, acc, sums, moved, m2m, c2e, check, zz, yy, xx, grouped_up,
     part, arrived, two, three, grouped, stacked, matrix, tail,
     load_sem, t_send, t_recv, b_send, b_recv, p_sem, a_send, a_recv, x_send, x_recv, z_send, z_recv,
 ):
@@ -287,10 +315,18 @@
     def exists(s, c):
         return (slab + s >= 0) & (slab + s < 4) & (col + c >= 0) & (col + c < 32)
 
-    main = pltpu.make_async_copy(m2l_ref.at[:, pl.ds(0, MAIN)], matrix, load_sem.at[0])
-    rest = pltpu.make_async_copy(m2l_ref.at[:, pl.ds(MAIN, REST)], tail, load_sem.at[1])
-    main.start()
-    rest.start()
+    first = pl.multiple_of(W * (35 * (3 - slab) - jnp.where(slab == 0, 4, 0)), W)
+    loads = [
+        pltpu.make_async_copy(positions_ref, positions, load_sem.at[0]),
+        pltpu.make_async_copy(charges_ref, charge, load_sem.at[1]),
+        pltpu.make_async_copy(c2e_ref, c2e_in, load_sem.at[2]),
+        pltpu.make_async_copy(m2m_ref, m2m_in, load_sem.at[3]),
+        pltpu.make_async_copy(m2l_ref.at[:, pl.ds(first, TILES * W)], matrix, load_sem.at[4]),
+        pltpu.make_async_copy(m2l_ref.at[:, pl.ds(LAST, REST)], tail, load_sem.at[5]),
+    ]
+    for load in loads:
+        load.start()
+
     targets[...] = jnp.zeros_like(targets)
     back[...] = jnp.zeros_like(back)
     two[:, :, 0:8, :] = jnp.zeros((4, 16, 8, W), F32)
@@ -307,14 +343,19 @@
         def _(s=s):
             pl.semaphore_signal(barrier, inc=1, device_id=(slab + s, col + outward), device_id_type=MESH)
 
+    three[...] = jnp.zeros_like(three)
+    acc[...] = jnp.zeros_like(acc)
+    stacked[...] = jnp.zeros_like(stacked)
+    check[NS:W, :] = jnp.zeros((W - NS, 8 * W), F32)
+    loads[0].wait()
+    loads[1].wait()
+    arrange_sources(positions, charge, moved)
     for row in range(8):
         for comp in range(3):
-            targets[row // 2 + 1, row % 2 + 1, comp * QT : (comp + 1) * QT, :] = src_ref[row, comp, 0:QT, :]
-    pad_matrices(c2e_ref, m2m_ref, c2e, m2m)
-    check[NS:W, :] = jnp.zeros((W - NS, 8 * W), F32)
-    shifted_sources(src_ref, moved)
-    acc[...] = jnp.zeros_like(acc)
-    three[...] = jnp.zeros_like(three)
+            targets[row // 2 + 1, row % 2 + 1, comp * QT : (comp + 1) * QT, :] = moved[1, row, comp, 0:QT, :]
+    loads[2].wait()
+    loads[3].wait()
+    pad_matrices(c2e_in, m2m_in, c2e, m2m)
 
     more = sum(jnp.where(exists(s, outward), 1, 0) for s in (-1, 0, 1))
     pl.semaphore_wait(barrier, len(others) + more)
@@ -353,7 +394,7 @@
 
     for_sides(lambda n, s, c: target_copy(n, s, c).start())
 
-    squares_and_checks(src_ref, check, zz, yy, xx)
+    squares_and_checks(moved.at[1], check, zz, yy, xx)
     part[...] = upward_two(check, c2e, m2m, grouped_up, low_y)
     theirs = pl.ds(pl.multiple_of(16 - 16 * low_y, 16), 16)
     pair_copy = pltpu.make_async_remote_copy(
@@ -367,7 +408,7 @@
     pair_copy.start()
 
     for_senders(lambda n, s, c: target_copy(n, s, c).wait_recv())
-    pair_loop(targets, moved, acc, 0, 2, 11, 0, 6, 1)
+    pair_loop(targets, moved, acc, 0, 1, 1, 0, 6)
 
     pair_copy.wait()
     mine = pl.ds(pl.multiple_of(16 * low_y, 16), 16)
@@ -397,12 +438,17 @@
 
     for k in range(1, 8):
         a_copy(k).start()
-    pair_loop(targets, moved, acc, 1, 10, 1, 0, 1, 5)
+    pair_loop(targets, moved, acc, 11, 1, 1, 0, 6)
     for k in range(1, 8):
         a_copy(k).wait()
     for k in range(1, 4):
         x_copy(k).start()
-    pair_loop(targets, moved, acc, 1, 10, 1, 5, 1, 5)
+    pair_loop(targets, moved, acc, 1, 10, 1, 0, 1)
+    for k in range(1, 4):
+        x_copy(k).wait()
+    for k in range(1, 4):
+        z_copy(k).start()
+    pair_loop(targets, moved, acc, 1, 10, 1, 5, 1)
 
     def reduce_halo(z, y):
         sum_rows(acc, sums, z, y)
@@ -414,11 +460,7 @@
         reduce_halo(z, 0)
         reduce_halo(z, 3)
     for_sides(lambda n, s, c: back_copy(n, s, c).start())
-    for k in range(1, 4):
-        x_copy(k).wait()
-    for k in range(1, 4):
-        z_copy(k).start()
-    pair_loop(targets, moved, acc, 1, 10, 1, 1, 4, 1)
+    pair_loop(targets, moved, acc, 1, 10, 1, 1, 4)
     for z in range(1, 5):
         for y in range(1, 3):
             sum_rows(acc, sums, z, y)
@@ -427,11 +469,9 @@
 
     densities_three(two, three, grouped, m2m)
     stack_sources(two, three, stacked, slab, col)
-    main.wait()
-    rest.wait()
-    total = jnp.transpose(translate(stacked, matrix, tail))
-    far2_ref[...] = total[:, 0:16]
-    far3_ref[...] = 0.5 * total[:, 16:18]
+    loads[4].wait()
+    loads[5].wait()
+    far[...] = jnp.transpose(translate(stacked, matrix, tail, first))
 
     for_senders(lambda n, s, c: back_copy(n, s, c).wait_recv())
     for z in range(4):
@@ -445,7 +485,6 @@
             row = (z * 2 + y) * 4
             for i in range(QT):
                 lines[row : row + 4, i * W : (i + 1) * W] = value[4 * i : 4 * i + 4]
-    interleave(lines, near_ref)
     for_sides(lambda n, s, c: target_copy(n, s, c).wait_send())
     for_sides(lambda n, s, c: back_copy(n, s, c).wait_send())
 
@@ -459,26 +498,26 @@
 
 
 def body(offsets, charges, check_to_equiv, m2m_matrix, m2l_matrix):
-    packed = jnp.concatenate([offsets, charges[:, :, None, :]], axis=2)
-    sources = jnp.swapaxes(packed.reshape(8, 4, W, Q), 2, 3)
     dma = pltpu.SemaphoreType.DMA
-    return pl.pallas_call(
+    lines, far = pl.pallas_call(
         whole_kernel,
         name="whole",
         out_shape=(
-            jax.ShapeDtypeStruct((4, 2, 4, W * QT), F32),
-            jax.ShapeDtypeStruct((NS, 16), F32),
-            jax.ShapeDtypeStruct((NS, 2), F32),
+            jax.ShapeDtypeStruct((32, W * QT), F32),
+            jax.ShapeDtypeStruct((24, NS), F32),
         ),
-        in_specs=[VMEM] * 3 + [pl.BlockSpec(memory_space=pl.ANY)],
-        out_specs=(VMEM, VMEM, VMEM),
+        in_specs=[pl.BlockSpec(memory_space=pl.ANY)] * 5,
+        out_specs=(VMEM, VMEM),
         scratch_shapes=[
+            scratch(4, 3, 2, W * Q),
+            scratch(4, 2, W * Q),
+            scratch(NS, NS),
+            scratch(NS, 8 * NS),
             scratch(6, 4, 16, W),
             scratch(6, 4, 16, W),
             scratch(6, 4, 16, 8, W),
             scratch(6, 4, 16, W),
             scratch(3, 8, 4, Q, W),
-            scratch(32, QT * W),
             scratch(W, 8 * W),
             scratch(W, W),
             scratch(W, 8 * W),
@@ -492,9 +531,9 @@
             scratch(2, 8, 40, W),
             scratch(256, 8 * W),
             scratch(24, (K_ALL + W - 1) // W * W),
-            scratch(NS, MAIN),
+            scratch(NS, TILES * W),
             scratch(NS, REST),
-            dma((2,)),
+            dma((6,)),
             dma((8,)),
             dma((8,)),
             dma((8,)),
@@ -511,7 +550,19 @@
             vmem_limit_bytes=58 * 1024 * 1024, collective_id=0, has_side_effects=True
         ),
         cost_estimate=pl.CostEstimate(flops=400000000, bytes_accessed=16000000, transcendentals=0),
-    )(sources, check_to_equiv, m2m_matrix, m2l_matrix)
+    )(jnp.swapaxes(offsets, 1, 2), charges, check_to_equiv, m2m_matrix, m2l_matrix)
+    near_field, far2, far3 = pl.pallas_call(
+        finish_kernel,
+        name="finish",
+        out_shape=(
+            jax.ShapeDtypeStruct((4, 2, 4, W * QT), F32),
+            jax.ShapeDtypeStruct((16, NS), F32),
+            jax.ShapeDtypeStruct((2, NS), F32),
+        ),
+        in_specs=[VMEM, VMEM],
+        out_specs=(VMEM, VMEM, VMEM),
+    )(lines, far)
+    return near_field, jnp.transpose(far2), jnp.transpose(far3)
 
 
 def solution(mesh):

time: 69.2 us -> 52 us (0.75)
  local copies, waits for them, and re-layouts: 8.41 us -> 0 us
  Pallas kernels: 58.8 us -> 51.1 us
  other arithmetic: 1.06 us -> 0 us
    pallas_call x1, Pallas kernels: 58.8 us -> 49.2 us  [body(): pl.pallas_call(whole_kernel, name='whole', out_shape=(jax.ShapeDtypeStruc...]
    pallas_call x2 -> x0, local copies, waits for them, and re-layouts: 2.92 us -> none  [body(): pl.pallas_call(whole_kernel, name='whole', out_shape=(jax.ShapeDtypeStruc...]
    concatenate x4 -> x0, local copies, waits for them, and re-layouts: 2.83 us -> none  [body(): packed = jnp.concatenate([offsets, charges[:, :, None, :]], axis=2)]
    unnamed x2 -> x0, local copies, waits for them, and re-layouts: 2.66 us -> none
    pallas_call x0 -> x1, Pallas kernels: none -> 1.94 us  [body(): pl.pallas_call(finish_kernel, name='finish', out_shape=(jax.ShapeDtypeStr...]
    transpose x1 -> x0, other arithmetic: 1.06 us -> none  [body(): sources = jnp.swapaxes(packed.reshape(8, 4, W, Q), 2, 3)]
where the time goes in v2:
time: 52 us; the launch traced here: 51.8 us
  Pallas kernels  51.1 us (98%)
  between operations  0.64 us (1%)
    pallas_call x1, Pallas kernels, body(): pl.pallas_call(whole_kernel, name='whole', out_shape=(jax.ShapeDtypeStruc...  49.2 us
    pallas_call x1, Pallas kernels, body(): pl.pallas_call(finish_kernel, name='finish', out_shape=(jax.ShapeDtypeStr...  1.94 us

profile of v2, /device:TPU:1, one launch (start us, length us, event | category | flops | bytes accessed | tf_op | source)
XLA Modules:
  0.0 51.8 jit_solution(10476710009642473973)
XLA Ops:
  0.6 49.2 %whole.1 = (f32[32,512]{1,0:T(8,128)}, f32[24,98]{1,0:T(8,128)}) custom-call(f32[4,3,2,8192]{3,2,1,0:T(2,128)} %bitcast.3, f32[4,2,8192]{2,1,0:T(2,128)} %charges_ref.1, f32[98,98]{1,0:T(8,128)} %c2e_ref.1, f32[98,784]{1,0:T(8,128)} %m2m_ref.1, f32[98,30968]{1,0:T(8,128)} %m2l_ref.1), custom_call_target="tpu_custom_call" | custom-call | flops 400000000 | bytes 16000000 | tf_op jit(solution)/shard_map/whole/pallas_call | solution.py:502
  49.8 1.9 %finish.1 = (f32[4,2,4,512]{3,2,1,0:T(4,128)}, f32[16,98]{1,0:T(8,128)}, f32[2,98]{1,0:T(2,128)}) custom-call(f32[32,512]{1,0:T(8,128)} %get-tuple-element.8.lines, f32[24,98]{1,0:T(8,128)} %get-tuple-element.9.far), custom_call_target="tpu_custom_call" | custom-call | tf_op jit(solution)/shard_map/finish/pallas_call | solution.py:554

commit v3 on v2

--- a/solution.py
+++ b/solution.py
@@ -176,22 +176,17 @@
     sums[z, y] = jnp.sum(acc[z, y], axis=1)
 
 
-def densities_three(two, three, grouped, m2m):
-    def gather(n, carry):
-        z, y = n // 8, n % 8
-        for bz in range(2):
-            for by in range(2):
-                for bx in range(2):
-                    octant = 4 * bz + 2 * by + bx
-                    grouped[pl.ds(pl.multiple_of(n * 16, 16), 16), octant * W : (octant + 1) * W] = two[
-                        2 * z + bz, 2 * y + by, pl.ds(8 + bx, 16, stride=2), :
-                    ]
-        return carry
-
-    lax.fori_loop(0, 16, gather, 0)
+def densities_three(two, three, grouped, m2m, zc):
+    for n in range(4):
+        z, y = n // 2, 2 * zc + n % 2
+        for octant in range(8):
+            bz, by, bx = octant // 4, octant // 2 % 2, octant % 2
+            grouped[n * 16 : (n + 1) * 16, octant * W : (octant + 1) * W] = two[
+                2 * z + bz, 2 * y + by, pl.ds(8 + bx, 16, stride=2), :
+            ]
     level_three = dot3(grouped[...], m2m[...], dot_t)
-    for n in range(16):
-        three[n // 8, n % 8, 8:24, :] = level_three[n * 16 : (n + 1) * 16]
+    for n in range(4):
+        three[n // 2, 2 * zc + n % 2, 8:24, :] = level_three[n * 16 : (n + 1) * 16]
 
 
 def stack_sources(two, three, stacked, slab, col):
@@ -297,6 +292,7 @@
     positions, charge, c2e_in, m2m_in, targets, back, acc, sums, moved, m2m, c2e, check, zz, yy, xx, grouped_up,
     part, arrived, two, three, grouped, stacked, matrix, tail,
     load_sem, t_send, t_recv, b_send, b_recv, p_sem, a_send, a_recv, x_send, x_recv, z_send, z_recv,
+    up_send, up_recv, down_send, down_recv,
 ):
     slab, col = lax.axis_index("slab"), lax.axis_index("col")
     zc, xc, low_y = col // 8, (col // 2) % 4, col % 2
@@ -329,6 +325,7 @@
 
     targets[...] = jnp.zeros_like(targets)
     back[...] = jnp.zeros_like(back)
+    three[...] = jnp.zeros_like(three)
     two[:, :, 0:8, :] = jnp.zeros((4, 16, 8, W), F32)
     two[:, :, 40:48, :] = jnp.zeros((4, 16, 8, W), F32)
 
@@ -343,7 +340,6 @@
         def _(s=s):
             pl.semaphore_signal(barrier, inc=1, device_id=(slab + s, col + outward), device_id_type=MESH)
 
-    three[...] = jnp.zeros_like(three)
     acc[...] = jnp.zeros_like(acc)
     stacked[...] = jnp.zeros_like(stacked)
     check[NS:W, :] = jnp.zeros((W - NS, 8 * W), F32)
@@ -430,44 +426,62 @@
         )
 
     def z_copy(k):
-        block = two.at[:, pl.ds(zc * 4, 4), 8:40]
+        block = three.at[:, pl.ds(2 * zc, 2), 8:24]
         return pltpu.make_async_remote_copy(
             src_ref=block, dst_ref=block, send_sem=z_send.at[k - 1], recv_sem=z_recv.at[k - 1],
             device_id=along_z(k), device_id_type=MESH,
         )
 
+    def row_copy(r, step):
+        send, recv = (up_send, up_recv) if step == 1 else (down_send, down_recv)
+        block = two.at[:, zc * 4 + r, 8:40]
+        return pltpu.make_async_remote_copy(
+            src_ref=block, dst_ref=block, send_sem=send.at[r], recv_sem=recv.at[r],
+            device_id=(slab, col + 8 * step), device_id_type=MESH,
+        )
+
+    def for_rows(act, sender):
+        for r in range(4):
+            if r > 0:
+                @pl.when((r > xc) & ((zc < 3) if sender else (zc > 0)))
+                def _(r=r):
+                    act(row_copy(r, 1))
+            if r < 3:
+                @pl.when((r < xc) & ((zc > 0) if sender else (zc < 3)))
+                def _(r=r):
+                    act(row_copy(r, -1))
+
     for k in range(1, 8):
         a_copy(k).start()
     pair_loop(targets, moved, acc, 11, 1, 1, 0, 6)
+    pair_loop(targets, moved, acc, 1, 10, 1, 0, 1)
     for k in range(1, 8):
         a_copy(k).wait()
     for k in range(1, 4):
         x_copy(k).start()
-    pair_loop(targets, moved, acc, 1, 10, 1, 0, 1)
+    pair_loop(targets, moved, acc, 1, 10, 1, 5, 1)
+    for y in range(4):
+        sum_rows(acc, sums, 0, y)
+        sum_rows(acc, sums, 5, y)
+    for z in range(1, 5):
+        sum_rows(acc, sums, z, 0)
+        sum_rows(acc, sums, z, 3)
+    for_sides(lambda n, s, c: back_copy(n, s, c).start())
+    pair_loop(targets, moved, acc, 1, 3, 1, 1, 4)
     for k in range(1, 4):
         x_copy(k).wait()
+    for_rows(lambda copy: copy.start(), True)
+    densities_three(two, three, grouped, m2m, zc)
     for k in range(1, 4):
         z_copy(k).start()
-    pair_loop(targets, moved, acc, 1, 10, 1, 5, 1)
-
-    def reduce_halo(z, y):
-        sum_rows(acc, sums, z, y)
-
-    for y in range(4):
-        reduce_halo(0, y)
-        reduce_halo(5, y)
-    for z in range(1, 5):
-        reduce_halo(z, 0)
-        reduce_halo(z, 3)
-    for_sides(lambda n, s, c: back_copy(n, s, c).start())
-    pair_loop(targets, moved, acc, 1, 10, 1, 1, 4)
+    pair_loop(targets, moved, acc, 4, 7, 1, 1, 4)
     for z in range(1, 5):
         for y in range(1, 3):
             sum_rows(acc, sums, z, y)
+    for_rows(lambda copy: copy.wait_recv(), False)
     for k in range(1, 4):
         z_copy(k).wait()
 
-    densities_three(two, three, grouped, m2m)
     stack_sources(two, three, stacked, slab, col)
     loads[4].wait()
     loads[5].wait()
@@ -485,6 +499,7 @@
             row = (z * 2 + y) * 4
             for i in range(QT):
                 lines[row : row + 4, i * W : (i + 1) * W] = value[4 * i : 4 * i + 4]
+    for_rows(lambda copy: copy.wait_send(), True)
     for_sides(lambda n, s, c: target_copy(n, s, c).wait_send())
     for_sides(lambda n, s, c: back_copy(n, s, c).wait_send())
 
@@ -529,7 +544,7 @@
             scratch(16, W),
             scratch(4, 16, 48, W),
             scratch(2, 8, 40, W),
-            scratch(256, 8 * W),
+            scratch(64, 8 * W),
             scratch(24, (K_ALL + W - 1) // W * W),
             scratch(NS, TILES * W),
             scratch(NS, REST),
@@ -545,6 +560,10 @@
             dma((3,)),
             dma((3,)),
             dma((3,)),
+            dma((4,)),
+            dma((4,)),
+            dma((4,)),
+            dma((4,)),
         ],
         compiler_params=pltpu.CompilerParams(
             vmem_limit_bytes=58 * 1024 * 1024, collective_id=0, has_side_effects=True

time: 52 us -> 44.7 us (0.86)
  Pallas kernels: 51.1 us -> 43.7 us
    pallas_call x1, Pallas kernels: 49.2 us -> 41.7 us  [body(): pl.pallas_call(whole_kernel, name='whole', out_shape=(jax.ShapeDtypeStruc...]
where the time goes in v3:
time: 44.7 us; the launch traced here: 44.3 us
  Pallas kernels  43.7 us (98%)
  between operations  0.64 us (1%)
    pallas_call x1, Pallas kernels, body(): pl.pallas_call(whole_kernel, name='whole', out_shape=(jax.ShapeDtypeStruc...  41.7 us
    pallas_call x1, Pallas kernels, body(): pl.pallas_call(finish_kernel, name='finish', out_shape=(jax.ShapeDtypeStr...  1.94 us

profile of v3, /device:TPU:1, one launch (start us, length us, event | category | flops | bytes accessed | tf_op | source)
XLA Modules:
  0.0 44.3 jit_solution(7287285187688524862)
XLA Ops:
  0.6 41.7 %whole.1 = (f32[32,512]{1,0:T(8,128)}, f32[24,98]{1,0:T(8,128)}) custom-call(f32[4,3,2,8192]{3,2,1,0:T(2,128)} %bitcast.3, f32[4,2,8192]{2,1,0:T(2,128)} %charges_ref.1, f32[98,98]{1,0:T(8,128)} %c2e_ref.1, f32[98,784]{1,0:T(8,128)} %m2m_ref.1, f32[98,30968]{1,0:T(8,128)} %m2l_ref.1), custom_call_target="tpu_custom_call" | custom-call | flops 400000000 | bytes 16000000 | tf_op jit(solution)/shard_map/whole/pallas_call | solution.py:517
  42.4 1.9 %finish.1 = (f32[4,2,4,512]{3,2,1,0:T(4,128)}, f32[16,98]{1,0:T(8,128)}, f32[2,98]{1,0:T(2,128)}) custom-call(f32[32,512]{1,0:T(8,128)} %get-tuple-element.8.lines, f32[24,98]{1,0:T(8,128)} %get-tuple-element.9.far), custom_call_target="tpu_custom_call" | custom-call | tf_op jit(solution)/shard_map/finish/pallas_call | solution.py:573

commit v4 on v3

--- a/solution.py
+++ b/solution.py
@@ -111,11 +111,11 @@
     return total
 
 
-def arrange_sources(positions, charge, moved):
+def arrange_sources(positions, charge, moved, z):
     lane = lax.broadcasted_iota(jnp.int32, (Q, W), 1)
 
-    def one(row, carry):
-        z, y = row // 2, row % 2
+    def one(y, carry):
+        row = 2 * z + y
         for comp in range(4):
             line = positions[z, comp, pl.ds(y, 1), :] if comp < 3 else charge[z, pl.ds(y, 1), :]
             turned = jnp.transpose(line.reshape(Q, W))
@@ -131,7 +131,7 @@
             moved[2, row, comp] = right
         return carry
 
-    lax.fori_loop(0, 8, one, 0)
+    lax.fori_loop(0, 2, one, 0)
 
 
 def pair_rows(t_ref, moved, acc, zs, ys, sz, sy):
@@ -169,7 +169,8 @@
         pair_rows(t_ref, moved, acc, iz // 3, iy // 3, 1 - iz % 3, 1 - iy % 3)
         return carry
 
-    lax.fori_loop(0, z_count * y_count, one, 0, unroll=2)
+    count = z_count * y_count
+    lax.fori_loop(0, count, one, 0, unroll=4 if count % 4 == 0 else count // 2)
 
 
 def sum_rows(acc, sums, z, y):
@@ -291,7 +292,7 @@
     positions_ref, charges_ref, c2e_ref, m2m_ref, m2l_ref, lines, far,
     positions, charge, c2e_in, m2m_in, targets, back, acc, sums, moved, m2m, c2e, check, zz, yy, xx, grouped_up,
     part, arrived, two, three, grouped, stacked, matrix, tail,
-    load_sem, t_send, t_recv, b_send, b_recv, p_sem, a_send, a_recv, x_send, x_recv, z_send, z_recv,
+    load_sem, t_send, t_recv, b_send, b_recv, p_sem, a_send, a_recv, z_send, z_recv,
     up_send, up_recv, down_send, down_recv,
 ):
     slab, col = lax.axis_index("slab"), lax.axis_index("col")
@@ -299,11 +300,8 @@
     place = slab * 2 + low_y
 
     def local_at(k):
-        to = lax.rem(place + k, 8)
-        return to // 2, (col // 2) * 2 + lax.rem(to, 2)
-
-    def along_x(k):
-        return slab, zc * 8 + lax.rem(xc + k, 4) * 2 + low_y
+        to = lax.rem(place + k % 8, 8)
+        return to // 2, zc * 8 + lax.rem(xc + k // 8, 4) * 2 + lax.rem(to, 2)
 
     def along_z(k):
         return slab, lax.rem(zc + k, 4) * 8 + xc * 2 + low_y
@@ -313,13 +311,16 @@
 
     first = pl.multiple_of(W * (35 * (3 - slab) - jnp.where(slab == 0, 4, 0)), W)
     loads = [
-        pltpu.make_async_copy(positions_ref, positions, load_sem.at[0]),
-        pltpu.make_async_copy(charges_ref, charge, load_sem.at[1]),
-        pltpu.make_async_copy(c2e_ref, c2e_in, load_sem.at[2]),
-        pltpu.make_async_copy(m2m_ref, m2m_in, load_sem.at[3]),
-        pltpu.make_async_copy(m2l_ref.at[:, pl.ds(first, TILES * W)], matrix, load_sem.at[4]),
-        pltpu.make_async_copy(m2l_ref.at[:, pl.ds(LAST, REST)], tail, load_sem.at[5]),
+        pltpu.make_async_copy(c2e_ref, c2e_in, load_sem.at[0]),
+        pltpu.make_async_copy(m2m_ref, m2m_in, load_sem.at[1]),
+        pltpu.make_async_copy(m2l_ref.at[:, pl.ds(first, TILES * W)], matrix, load_sem.at[2]),
+        pltpu.make_async_copy(m2l_ref.at[:, pl.ds(LAST, REST)], tail, load_sem.at[3]),
     ]
+    rows_in = [pltpu.make_async_copy(positions_ref.at[z], positions.at[z], load_sem.at[4 + z]) for z in range(4)]
+    charges_in = [pltpu.make_async_copy(charges_ref.at[z], charge.at[z], load_sem.at[8 + z]) for z in range(4)]
+    for z in range(4):
+        rows_in[z].start()
+        charges_in[z].start()
     for load in loads:
         load.start()
 
@@ -330,8 +331,8 @@
     two[:, :, 40:48, :] = jnp.zeros((4, 16, 8, W), F32)
 
     barrier = pltpu.get_barrier_semaphore()
-    others = [local_at(k) for k in range(1, 8)]
-    others += [along_x(k) for k in range(1, 4)] + [along_z(k) for k in range(1, 4)]
+    others = [local_at(k) for k in range(1, 32)]
+    others += [along_z(k) for k in range(1, 4)]
     for other in others:
         pl.semaphore_signal(barrier, inc=1, device_id=other, device_id_type=MESH)
     outward = 2 * low_y - 1
@@ -343,14 +344,15 @@
     acc[...] = jnp.zeros_like(acc)
     stacked[...] = jnp.zeros_like(stacked)
     check[NS:W, :] = jnp.zeros((W - NS, 8 * W), F32)
-    loads[0].wait()
-    loads[1].wait()
-    arrange_sources(positions, charge, moved)
+    for z in range(4):
+        rows_in[z].wait()
+        charges_in[z].wait()
+        arrange_sources(positions, charge, moved, z)
     for row in range(8):
         for comp in range(3):
             targets[row // 2 + 1, row % 2 + 1, comp * QT : (comp + 1) * QT, :] = moved[1, row, comp, 0:QT, :]
-    loads[2].wait()
-    loads[3].wait()
+    loads[0].wait()
+    loads[1].wait()
     pad_matrices(c2e_in, m2m_in, c2e, m2m)
 
     more = sum(jnp.where(exists(s, outward), 1, 0) for s in (-1, 0, 1))
@@ -418,13 +420,6 @@
             device_id=local_at(k), device_id_type=MESH,
         )
 
-    def x_copy(k):
-        block = two.at[:, col // 2, 8:40]
-        return pltpu.make_async_remote_copy(
-            src_ref=block, dst_ref=block, send_sem=x_send.at[k - 1], recv_sem=x_recv.at[k - 1],
-            device_id=along_x(k), device_id_type=MESH,
-        )
-
     def z_copy(k):
         block = three.at[:, pl.ds(2 * zc, 2), 8:24]
         return pltpu.make_async_remote_copy(
@@ -451,14 +446,10 @@
                 def _(r=r):
                     act(row_copy(r, -1))
 
-    for k in range(1, 8):
+    for k in range(1, 32):
         a_copy(k).start()
     pair_loop(targets, moved, acc, 11, 1, 1, 0, 6)
     pair_loop(targets, moved, acc, 1, 10, 1, 0, 1)
-    for k in range(1, 8):
-        a_copy(k).wait()
-    for k in range(1, 4):
-        x_copy(k).start()
     pair_loop(targets, moved, acc, 1, 10, 1, 5, 1)
     for y in range(4):
         sum_rows(acc, sums, 0, y)
@@ -467,14 +458,13 @@
         sum_rows(acc, sums, z, 0)
         sum_rows(acc, sums, z, 3)
     for_sides(lambda n, s, c: back_copy(n, s, c).start())
-    pair_loop(targets, moved, acc, 1, 3, 1, 1, 4)
-    for k in range(1, 4):
-        x_copy(k).wait()
+    for k in range(1, 32):
+        a_copy(k).wait()
     for_rows(lambda copy: copy.start(), True)
     densities_three(two, three, grouped, m2m, zc)
     for k in range(1, 4):
         z_copy(k).start()
-    pair_loop(targets, moved, acc, 4, 7, 1, 1, 4)
+    pair_loop(targets, moved, acc, 1, 10, 1, 1, 4)
     for z in range(1, 5):
         for y in range(1, 3):
             sum_rows(acc, sums, z, y)
@@ -483,8 +473,8 @@
         z_copy(k).wait()
 
     stack_sources(two, three, stacked, slab, col)
-    loads[4].wait()
-    loads[5].wait()
+    loads[2].wait()
+    loads[3].wait()
     far[...] = jnp.transpose(translate(stacked, matrix, tail, first))
 
     for_senders(lambda n, s, c: back_copy(n, s, c).wait_recv())
@@ -548,16 +538,14 @@
             scratch(24, (K_ALL + W - 1) // W * W),
             scratch(NS, TILES * W),
             scratch(NS, REST),
-            dma((6,)),
+            dma((12,)),
             dma((8,)),
             dma((8,)),
             dma((8,)),
             dma((8,)),
             dma((2,)),
-            dma((7,)),
-            dma((7,)),
-            dma((3,)),
-            dma((3,)),
+            dma((31,)),
+            dma((31,)),
             dma((3,)),
             dma((3,)),
             dma((4,)),

time: 44.7 us -> 43.9 us (0.982)
  Pallas kernels: 43.7 us -> 43.1 us
    pallas_call x1, Pallas kernels: 41.7 us -> 41.1 us  [body(): pl.pallas_call(whole_kernel, name='whole', out_shape=(jax.ShapeDtypeStruc...]
where the time goes in v4:
time: 43.9 us; the launch traced here: 43.7 us
  Pallas kernels  43.1 us (98%)
  between operations  0.64 us (1%)
    pallas_call x1, Pallas kernels, body(): pl.pallas_call(whole_kernel, name='whole', out_shape=(jax.ShapeDtypeStruc...  41.1 us
    pallas_call x1, Pallas kernels, body(): pl.pallas_call(finish_kernel, name='finish', out_shape=(jax.ShapeDtypeStr...  1.94 us

profile of v4, /device:TPU:1, one launch (start us, length us, event | category | flops | bytes accessed | tf_op | source)
XLA Modules:
  0.0 43.7 jit_solution(15668843395764379241)
XLA Ops:
  0.6 41.1 %whole.1 = (f32[32,512]{1,0:T(8,128)}, f32[24,98]{1,0:T(8,128)}) custom-call(f32[4,3,2,8192]{3,2,1,0:T(2,128)} %bitcast.3, f32[4,2,8192]{2,1,0:T(2,128)} %charges_ref.1, f32[98,98]{1,0:T(8,128)} %c2e_ref.1, f32[98,784]{1,0:T(8,128)} %m2m_ref.1, f32[98,30968]{1,0:T(8,128)} %m2l_ref.1), custom_call_target="tpu_custom_call" | custom-call | flops 400000000 | bytes 16000000 | tf_op jit(solution)/shard_map/whole/pallas_call | solution.py:507
  41.8 1.9 %finish.1 = (f32[4,2,4,512]{3,2,1,0:T(4,128)}, f32[16,98]{1,0:T(8,128)}, f32[2,98]{1,0:T(2,128)}) custom-call(f32[32,512]{1,0:T(8,128)} %get-tuple-element.8.lines, f32[24,98]{1,0:T(8,128)} %get-tuple-element.9.far), custom_call_target="tpu_custom_call" | custom-call | tf_op jit(solution)/shard_map/finish/pallas_call | solution.py:561

commit v5 on v4

--- a/solution.py
+++ b/solution.py
@@ -429,7 +429,7 @@
 
     def row_copy(r, step):
         send, recv = (up_send, up_recv) if step == 1 else (down_send, down_recv)
-        block = two.at[:, zc * 4 + r, 8:40]
+        block = two.at[:, zc * 4 + r, pl.ds(pl.multiple_of(8 + 8 * low_y, 8), 24)]
         return pltpu.make_async_remote_copy(
             src_ref=block, dst_ref=block, send_sem=send.at[r], recv_sem=recv.at[r],
             device_id=(slab, col + 8 * step), device_id_type=MESH,
@@ -458,13 +458,14 @@
         sum_rows(acc, sums, z, 0)
         sum_rows(acc, sums, z, 3)
     for_sides(lambda n, s, c: back_copy(n, s, c).start())
+    pair_loop(targets, moved, acc, 1, 2, 1, 1, 4)
     for k in range(1, 32):
         a_copy(k).wait()
     for_rows(lambda copy: copy.start(), True)
     densities_three(two, three, grouped, m2m, zc)
     for k in range(1, 4):
         z_copy(k).start()
-    pair_loop(targets, moved, acc, 1, 10, 1, 1, 4)
+    pair_loop(targets, moved, acc, 3, 8, 1, 1, 4)
     for z in range(1, 5):
         for y in range(1, 3):
             sum_rows(acc, sums, z, y)

time: 43.9 us -> 42.9 us (0.977)
  Pallas kernels: 43.1 us -> 42.1 us
    pallas_call x1, Pallas kernels: 41.1 us -> 40.1 us  [body(): pl.pallas_call(whole_kernel, name='whole', out_shape=(jax.ShapeDtypeStruc...]
where the time goes in v5:
time: 42.9 us; the launch traced here: 42.7 us
  Pallas kernels  42.1 us (98%)
  between operations  0.64 us (1%)
    pallas_call x1, Pallas kernels, body(): pl.pallas_call(whole_kernel, name='whole', out_shape=(jax.ShapeDtypeStruc...  40.1 us
    pallas_call x1, Pallas kernels, body(): pl.pallas_call(finish_kernel, name='finish', out_shape=(jax.ShapeDtypeStr...  1.94 us

profile of v5, /device:TPU:1, one launch (start us, length us, event | category | flops | bytes accessed | tf_op | source)
XLA Modules:
  0.0 42.7 jit_solution(15539658302457464779)
XLA Ops:
  0.6 40.1 %whole.1 = (f32[32,512]{1,0:T(8,128)}, f32[24,98]{1,0:T(8,128)}) custom-call(f32[4,3,2,8192]{3,2,1,0:T(2,128)} %bitcast.3, f32[4,2,8192]{2,1,0:T(2,128)} %charges_ref.1, f32[98,98]{1,0:T(8,128)} %c2e_ref.1, f32[98,784]{1,0:T(8,128)} %m2m_ref.1, f32[98,30968]{1,0:T(8,128)} %m2l_ref.1), custom_call_target="tpu_custom_call" | custom-call | flops 400000000 | bytes 16000000 | tf_op jit(solution)/shard_map/whole/pallas_call | solution.py:508
  40.8 1.9 %finish.1 = (f32[4,2,4,512]{3,2,1,0:T(4,128)}, f32[16,98]{1,0:T(8,128)}, f32[2,98]{1,0:T(2,128)}) custom-call(f32[32,512]{1,0:T(8,128)} %get-tuple-element.8.lines, f32[24,98]{1,0:T(8,128)} %get-tuple-element.9.far), custom_call_target="tpu_custom_call" | custom-call | tf_op jit(solution)/shard_map/finish/pallas_call | solution.py:562
